TPU v7x, 256 devices: a whole 4x4x8 slice. The times are simulated.
256 devices in a mesh: dom: 32 (over z, y), sub: 8 (over x, core).
Axes of the slice: x: 4, y: 4, z: 8, core: 2. Of those that a mesh axis runs over, the one named last changes fastest.
Arguments:
- node: bfloat16 [32, 8, 512, 128], P('dom', 'sub'), may hold values from -6 to 6
- edges: bfloat16 [32, 8, 2048, 128], P('dom', 'sub'), may hold values from -6 to 6
- edge_src: int32 [32, 8, 2048], P('dom', 'sub'), may hold values from 0 to 703, as said below
- edge_dst: int32 [32, 8, 2048], P('dom', 'sub'), may hold values from 0 to 511, as said below
- edge_count: int32 [32, 8], P('dom', 'sub'), may hold values from 768 to 2048, as said below
- intra_idx: int32 [32, 8, 8, 8], P('dom', 'sub'), may hold values from 0 to 511, as said below
- bound_idx: int32 [32, 8, 2, 16], P('dom', 'sub'), may hold values from 0 to 511, as said below
- cross_pick: int32 [8, 2, 8, 8], P('sub'), may hold values from 0 to 15, as said below
- match_send: int32 [32, 8, 8, 16], P('dom', 'sub'), may hold values from 0 to 511, as said below
- pool_first: int32 [32, 8, 256], P('dom', 'sub'), may hold values from 0 to 511, as said below
- pool_second: int32 [32, 8, 256], P('dom', 'sub'), may hold values from 0 to 639, as said below
- edge_w1: bfloat16 [384, 128], replicated, may hold values from -0.3125 to 0.3125
- edge_b1: float32 [128], replicated, may hold values from -3 to 3
- edge_w2: bfloat16 [128, 128], replicated, may hold values from -0.5 to 0.5
- edge_gain: float32 [128], replicated, may hold values from 0.25 to 1.75
- node_w1: bfloat16 [256, 128], replicated, may hold values from -0.375 to 0.375
- node_b1: float32 [128], replicated, may hold values from -3 to 3
- node_w2: bfloat16 [128, 128], replicated, may hold values from -0.5 to 0.5
- node_gain: float32 [128], replicated, may hold values from 0.25 to 1.75
- edge_cot: bfloat16 [32, 8, 2048, 128], P('dom', 'sub'), may hold values from -8 to 8
- coarse_cot: bfloat16 [32, 8, 256, 128], P('dom', 'sub'), may hold values from -8 to 8
Outputs:
- new_edges: bfloat16 [32, 8, 2048, 128], P('dom', 'sub')
- coarse: bfloat16 [32, 8, 256, 128], P('dom', 'sub')
- d_node: float32 [32, 8, 512, 128], P('dom', 'sub')
- d_edges: bfloat16 [32, 8, 2048, 128], P('dom', 'sub')
- grad_edge_w1: float32 [384, 128], replicated
- grad_edge_b1: float32 [128], replicated
- grad_edge_w2: float32 [128, 128], replicated
- grad_edge_gain: float32 [128], replicated
- grad_node_w1: float32 [256, 128], replicated
- grad_node_b1: float32 [128], replicated
- grad_node_w2: float32 [128, 128], replicated
- grad_node_gain: float32 [128], replicated
Inputs may be any that keep to these rules, and one draw needn't show every extreme that they name: `edge_src`: edges of slab 0 never refer to kind 1 row and edges of the last slab never to kind 2 rows. `edge_dst`: Non-decreasing along each device's slots. `edge_count`: A multiple of 128; some device in every draw has all 2048 slots live. `intra_idx`: distinct within each list. `bound_idx`: all 32 cells of a device are distinct. `cross_pick`: for each s and k, every face position appears exactly 4 times over the 8 x 8 entries; the same on every slab. `match_send`: together with pool_first and pool_second every cell of every device belongs to exactly one coarse cell. `pool_first`: never a cell listed in the device's match_send. `pool_second`: values of 512 or more name received rows, each exactly once.
All inputs are finite; a program needn't handle non-finite values.
Results may differ from a plain program's by a relative error of at most 0.0062.
Values may be sent and summed in bfloat16 or wider, within the bound.
No kernel may reach another device: no remote copies, remote signals or barrier semaphores. Data moves between devices by JAX's collectives and lax.ppermute only.
A program may use at most 64 MiB of HBM per device.

v0:
```python
import math

import jax
import jax.numpy as jnp
from jax import lax
from jax.sharding import PartitionSpec as P

NORM_EPSILON = 1e-05


def with_halo(cells, sides, width):
    for axis, dim in sides:
        count = lax.axis_size(axis)
        ends = count - 1
        head = lax.slice_in_dim(cells, 0, width, axis=dim)
        tail = lax.slice_in_dim(cells, cells.shape[dim] - width, cells.shape[dim], axis=dim)
        cells = jnp.concatenate(
            [
                lax.ppermute(tail, axis, [(i, (i + 1) % count) for i in range(ends)]),
                cells,
                lax.ppermute(head, axis, [((i + 1) % count, i) for i in range(ends)]),
            ],
            axis=dim,
        )
    return cells


def layer_norm(values, gain_vec):
    average = jnp.mean(values, axis=-1, keepdims=True)
    centred = values - average
    variance = jnp.mean(centred * centred, axis=-1, keepdims=True)
    inv_std = lax.rsqrt(variance + NORM_EPSILON)
    normed = centred * inv_std
    return (normed * gain_vec, normed, inv_std)


def norm_backward(upstream, normed, inv_std, gain_vec):
    scaled = upstream * gain_vec
    inner = (
        scaled
        - jnp.mean(scaled, axis=-1, keepdims=True)
        - normed * jnp.mean(scaled * normed, axis=-1, keepdims=True)
    )
    return (inner * inv_std, jnp.sum(upstream * normed, axis=0))


def mlp_forward(inputs, first_w, first_b, second_w, gain_vec):
    pre_act = jnp.dot(inputs, first_w, preferred_element_type=jnp.float32) + first_b
    activation = jax.nn.silu(pre_act).astype(jnp.bfloat16)
    projected = jnp.dot(activation, second_w, preferred_element_type=jnp.float32)
    result, normed, inv_std = layer_norm(projected, gain_vec)
    return (result, (pre_act, activation, normed, inv_std))


def mlp_backward(upstream, inputs, saved_vals, first_w, second_w, gain_vec):
    pre_act, activation, normed, inv_std = saved_vals
    d_projected, d_gain = norm_backward(upstream, normed, inv_std, gain_vec)
    d_proj_half = d_projected.astype(jnp.bfloat16)
    d_second = jnp.dot(activation.T, d_proj_half, preferred_element_type=jnp.float32)
    d_activation = jnp.dot(d_proj_half, second_w.T, preferred_element_type=jnp.float32)
    sigmoid_pre = jax.nn.sigmoid(pre_act)
    d_pre = d_activation * sigmoid_pre * (1.0 + pre_act * (1.0 - sigmoid_pre))
    d_pre_half = d_pre.astype(jnp.bfloat16)
    d_first = jnp.dot(inputs.T, d_pre_half, preferred_element_type=jnp.float32)
    d_inputs = jnp.dot(d_pre_half, first_w.T, preferred_element_type=jnp.float32)
    return (d_inputs, (d_first, jnp.sum(d_pre, axis=0), d_second, d_gain))


def layer_forward(node_here, row_table, edge_here, source_ids, target_ids, live_count, weights):
    edge_w1, edge_b1, edge_w2, edge_gain, node_w1, node_b1, node_w2, node_gain = weights
    cell_count = node_here.shape[0]
    live_mask = (jnp.arange(edge_here.shape[0]) < live_count)[:, None]
    edge_inputs = jnp.concatenate(
        [
            edge_here,
            jnp.take(row_table, source_ids, axis=0),
            jnp.take(node_here, target_ids, axis=0),
        ],
        axis=1,
    )
    message, edge_saved = mlp_forward(edge_inputs, edge_w1, edge_b1, edge_w2, edge_gain)
    message = jnp.where(live_mask, message, 0.0)
    new_edge = jnp.where(live_mask, edge_here.astype(jnp.float32) + message, 0.0).astype(
        jnp.bfloat16
    )
    aggregate = jax.ops.segment_sum(
        message, target_ids, num_segments=cell_count, indices_are_sorted=True
    ).astype(jnp.bfloat16)
    node_inputs = jnp.concatenate([node_here, aggregate], axis=1)
    update, node_saved = mlp_forward(node_inputs, node_w1, node_b1, node_w2, node_gain)
    fresh = (node_here.astype(jnp.float32) + update).astype(jnp.bfloat16)
    return (new_edge, fresh, (live_mask, edge_inputs, edge_saved, node_inputs, node_saved))


def layer_backward(saved, d_fresh, edge_cot_here, target_ids, source_ids, table_rows, weights):
    edge_w1, edge_b1, edge_w2, edge_gain, node_w1, node_b1, node_w2, node_gain = weights
    live_mask, edge_inputs, edge_saved, node_inputs, node_saved = saved
    cell_count, feature = d_fresh.shape
    d_node_in, node_grads = mlp_backward(
        d_fresh, node_inputs, node_saved, node_w1, node_w2, node_gain
    )
    cot_here = jnp.where(live_mask, edge_cot_here.astype(jnp.float32), 0.0)
    d_message = jnp.where(
        live_mask, cot_here + jnp.take(d_node_in[:, feature:], target_ids, axis=0), 0.0
    )
    d_edge_in, edge_grads = mlp_backward(
        d_message, edge_inputs, edge_saved, edge_w1, edge_w2, edge_gain
    )
    d_edge = (cot_here + d_edge_in[:, :feature]).astype(jnp.bfloat16)
    d_node = (
        d_fresh
        + d_node_in[:, :feature]
        + jax.ops.segment_sum(
            d_edge_in[:, 2 * feature :],
            target_ids,
            num_segments=cell_count,
            indices_are_sorted=True,
        )
    )
    d_table = jax.ops.segment_sum(
        d_edge_in[:, feature : 2 * feature], source_ids, num_segments=table_rows
    )
    d_node = d_node + d_table[:cell_count]
    return (d_edge, d_node, d_table[cell_count:], edge_grads + node_grads)


def per_device(
    node,
    edges,
    edge_src,
    edge_dst,
    edge_count,
    intra_idx,
    bound_idx,
    cross_pick,
    match_send,
    pool_first,
    pool_second,
    edge_w1,
    edge_b1,
    edge_w2,
    edge_gain,
    node_w1,
    node_b1,
    node_w2,
    node_gain,
    edge_cot,
    coarse_cot,
):
    weights = (edge_w1, edge_b1, edge_w2, edge_gain, node_w1, node_b1, node_w2, node_gain)
    node_here = node[0, 0]
    cell_count, feature = node_here.shape
    peer_count = lax.axis_size("sub")
    intra_ids = intra_idx[0, 0]
    halo_rows = intra_ids.shape[1]
    face_ids = bound_idx[0, 0]
    pick_ids = cross_pick[0]
    intra_rows = jnp.take(node_here, intra_ids, axis=0)
    face_cells = jnp.stack([jnp.take(face_ids[0], pick_ids[0]), jnp.take(face_ids[1], pick_ids[1])])
    face_rows = jnp.take(node_here, face_cells, axis=0)
    arrived = with_halo(face_rows, (("dom", 0),), 1)
    from_below = arrived[0]
    from_above = arrived[3]
    received = lax.all_to_all(
        jnp.stack([intra_rows, from_below, from_above]),
        "sub",
        split_axis=1,
        concat_axis=1,
        tiled=True,
    )
    row_table = jnp.concatenate([node_here, received.reshape(-1, feature)], axis=0)
    source_ids = edge_src[0, 0]
    target_ids = edge_dst[0, 0]
    new_edge, fresh, saved = layer_forward(
        node_here, row_table, edges[0, 0], source_ids, target_ids, edge_count[0, 0], weights
    )
    match_ids = match_send[0, 0]
    partners = lax.all_to_all(
        jnp.take(fresh, match_ids, axis=0), "sub", split_axis=0, concat_axis=0, tiled=True
    )
    pool_table = jnp.concatenate([fresh, partners.reshape(-1, feature)], axis=0)
    first_ids = pool_first[0, 0]
    second_ids = pool_second[0, 0]
    coarse = (
        0.5
        * (
            jnp.take(fresh, first_ids, axis=0).astype(jnp.float32)
            + jnp.take(pool_table, second_ids, axis=0).astype(jnp.float32)
        )
    ).astype(jnp.bfloat16)
    half_grad = 0.5 * coarse_cot[0, 0].astype(jnp.float32)
    d_pool = jnp.zeros(pool_table.shape, jnp.float32).at[second_ids].add(half_grad)
    d_fresh = jnp.zeros(fresh.shape, jnp.float32).at[first_ids].add(half_grad) + d_pool[:cell_count]
    returned = lax.all_to_all(
        d_pool[cell_count:].reshape(peer_count, -1, feature).astype(jnp.bfloat16),
        "sub",
        split_axis=0,
        concat_axis=0,
        tiled=True,
    ).astype(jnp.float32)
    d_fresh = d_fresh.at[match_ids.reshape(-1)].add(returned.reshape(-1, feature))
    d_edge, d_node, d_halo, grads = layer_backward(
        saved, d_fresh, edge_cot[0, 0], target_ids, source_ids, row_table.shape[0], weights
    )
    d_sent = lax.all_to_all(
        d_halo.reshape(3, peer_count, halo_rows, feature).astype(jnp.bfloat16),
        "sub",
        split_axis=1,
        concat_axis=1,
        tiled=True,
    ).astype(jnp.float32)
    d_node = d_node.at[intra_ids.reshape(-1)].add(d_sent[0].reshape(-1, feature))
    coming_back = with_halo(
        jnp.stack([d_sent[1], d_sent[2]]).astype(jnp.bfloat16), (("dom", 0),), 1
    ).astype(jnp.float32)
    d_node = d_node.at[face_cells[0].reshape(-1)].add(coming_back[0].reshape(-1, feature))
    d_node = d_node.at[face_cells[1].reshape(-1)].add(coming_back[3].reshape(-1, feature))
    totals = lax.psum(
        (grads[0], grads[1], grads[2], grads[3], grads[4], grads[5], grads[6], grads[7]),
        ("dom", "sub"),
    )
    grad_scale = 1.0 / math.sqrt(lax.axis_size("dom") * lax.axis_size("sub") * edges.shape[2])
    return (
        new_edge[None, None],
        coarse[None, None],
        d_node[None, None],
        d_edge[None, None],
        totals[0] * grad_scale,
        totals[1] * grad_scale,
        totals[2] * grad_scale,
        totals[3] * grad_scale,
        totals[4] * grad_scale,
        totals[5] * grad_scale,
        totals[6] * grad_scale,
        totals[7] * grad_scale,
    )


def solution(mesh):
    return jax.shard_map(
        per_device,
        mesh=mesh,
        in_specs=(
            P("dom", "sub", None, None),
            P("dom", "sub", None, None),
            P("dom", "sub", None),
            P("dom", "sub", None),
            P("dom", "sub"),
            P("dom", "sub", None, None),
            P("dom", "sub", None, None),
            P("sub", None, None, None),
            P("dom", "sub", None, None),
            P("dom", "sub", None),
            P("dom", "sub", None),
            P(),
            P(),
            P(),
            P(),
            P(),
            P(),
            P(),
            P(),
            P("dom", "sub", None, None),
            P("dom", "sub", None, None),
        ),
        out_specs=(
            P("dom", "sub", None, None),
            P("dom", "sub", None, None),
            P("dom", "sub", None, None),
            P("dom", "sub", None, None),
            P(),
            P(),
            P(),
            P(),
            P(),
            P(),
            P(),
            P(),
        ),
        check_vma=False,
    )
```

profile of v0, /device:TPU:1, one launch (start us, length us, event | category | flops | bytes accessed | tf_op | source)
XLA Modules:
  0.0 489.4 jit_solution(7662810568325433846)
XLA Ops:
  11.7 4.0 collective-permute-start
  17.0 1.5 scatter_custom_fusion.1
  19.2 5.2 %all-to-all-start.2 = ((bf16[8,16,128]{2,1,0:T(8,128)(2,1)}), bf16[8,16,128]{2,1,0:T(8,128)(2,1)S(1)}, u32[]{:S(2)}, u32[]{:S(2)}) async-start(bf16[8,16,128]{2,1,0:T(8,128)(2,1)} %bitcast.41), calls=%async_computation.2 | async-start | bytes 65536 | tf_op jit(solution)/shard_map/all_to_all | solution.py:194
  30.5 4.8 all-to-all-start
  35.5 2.1 scatter_custom_fusion.2
  38.0 6.2 %gather_fusion.3 = bf16[2048,128]{1,0:T(8,128)(2,1)S(1)} fusion(bf16[512,128]{1,0:T(8,128)(2,1)S(1)} %bitcast.155, s32[2048]{0:T(1024)S(1)} %broadcast_clamp_fusion), kind=kCustom, calls=%fused_computation.5 | custom fusion | bytes 1056768 | tf_op jit(solution)/shard_map/jit(_take)/gather | solution.py:77
  46.7 6.2 %gather_fusion.2 = bf16[2048,128]{1,0:T(8,128)(2,1)S(1)} fusion(bf16[704,128]{1,0:T(8,128)(2,1)S(1)} %copy.92, s32[2048]{0:T(1024)S(1)} %broadcast_clamp_fusion.1), kind=kCustom, calls=%fused_computation.4 | custom fusion | bytes 1056768 | tf_op jit(solution)/shard_map/jit(_take)/gather | solution.py:76
  55.2 1.7 multiply_convert_fusion.1
  57.7 2.2 fusion.11
  61.2 12.9 %scatter_custom_fusion = f32[512,128]{1,0:T(8,128)S(1)} fusion(s32[2048]{0:T(1024)S(1)} %bitcast.175, f32[2048,128]{1,0:T(8,128)} %copy.96, f32[]{:T(128)} %constant.113.clone.1), kind=kCustom, calls=%fused_computation.76 | custom fusion | flops 262144 | bytes 262656 | tf_op jit(solution)/shard_map/scatter-add | solution.py:86
  79.3 7.6 %gather_fusion.7 = f32[2048,128]{1,0:T(8,128)} fusion(f32[512,128]{1,0:T(8,128)S(1)} %slice.118, s32[2048]{0:T(1024)S(1)} %broadcast_clamp_fusion), kind=kCustom, calls=%fused_computation.9 | custom fusion | bytes 2105344 | tf_op jit(solution)/shard_map/jit(_take)/gather | solution.py:104
  86.8 1.6 copy.104
  94.1 1.6 fusion.14
  95.7 12.2 %scatter_custom_fusion.4 = f32[704,128]{1,0:T(8,128)} fusion(s32[2048]{0:T(1024)S(1)} %bitcast.172, f32[2048,384]{1,0:T(8,128)S(1)} %fusion.14, f32[]{:T(128)} %constant.113.clone.1), kind=kCustom, calls=%fused_computation.28 | custom fusion | flops 262144 | bytes 1409028 | tf_op jit(solution)/shard_map/scatter-add | solution.py:120
  110.5 4.8 all-to-all-start.1
  115.3 81.9 %all-reduce = (f32[128]{0:T(128)S(1)}, f32[128]{0:T(128)S(1)}, f32[128]{0:T(128)S(1)}, f32[128]{0:T(128)S(1)}) all-reduce(f32[128]{0:T(128)} %get-tuple-element.85, f32[128]{0:T(128)S(1)} %copy-done.34, f32[128]{0:T(128)} %get-tuple-element.87, f32[128]{0:T(128)} %get-tuple-element.52), channel_id=1, replica_groups=mesh['dom'=32,'sub'=8] {'dom','sub'}, use_global_device_ids=true, to_apply=%region_19.21 | all-reduce | flops 512 | bytes 4096 | tf_op jit(solution)/shard_map/psum | solution.py:218
  198.8 1.8 slice_add_fusion
  200.6 2.6 copy.121
  203.2 2.3 fusion.12
  206.9 2.0 copy.112
  208.9 1.6 gather_fusion.4
  211.2 14.1 %scatter_custom_fusion.5 = f32[512,128]{1,0:T(8,128)} fusion(f32[512,128]{1,0:T(8,128)} %slice_add_fusion, s32[2048]{0:T(1024)} %bitcast.173, f32[2048,384]{1,0:T(8,128)S(1)} %fusion.14), kind=kCustom, calls=%fused_computation.26 | custom fusion | flops 262144 | bytes 1310720 | tf_op jit(solution)/shard_map/scatter-add | solution.py:113
  225.3 2.1 copy.113
  227.4 4.3 all-to-all-start.3
  233.7 2.7 all-to-all-done.3
  236.5 2.3 collective-permute-start.2
  242.1 1.6 collective-permute-done.3
  246.0 230.3 %all-reduce.4.cloned.1.call-done = (f32[384,128]{1,0:T(8,128)}, f32[128,128]{1,0:T(8,128)}, f32[256,128]{1,0:T(8,128)}, f32[128,128]{1,0:T(8,128)}) async-done(((f32[384,128]{1,0:T(8,128)}, f32[128,128]{1,0:T(8,128)}, f32[256,128]{1,0:T(8,128)}, f32[128,128]{1,0:T(8,128)}), (f32[384,128]{1,0:T(8,128)}, f32[128,128]{1,0:T(8,128)}, f32[256,128]{1,0:T(8,128)}, ...) | async-done | bytes 458768 | tf_op jit(solution)/shard_map/psum | solution.py:218
  476.4 1.6 broadcast_multiply_fusion
  478.0 1.5 broadcast_multiply_fusion.3
  479.5 1.5 broadcast_multiply_fusion.2
  480.9 1.6 broadcast_multiply_fusion.1
  (200 shorter events, 43.4 us)
Async XLA Ops:
  7.2 47.9 %copy-start = (bf16[384,128]{1,0:T(8,128)(2,1)S(1)}, bf16[384,128]{1,0:T(8,128)(2,1)}, u32[]{:S(2)}) copy-start(bf16[384,128]{1,0:T(8,128)(2,1)} %param.34) | copy-start | bytes 294916
  9.6 7.4 %copy-start.17 = (bf16[1,1,256,128]{3,2,1,0:T(8,128)(2,1)S(1)}, bf16[1,1,256,128]{3,2,1,0:T(8,128)(2,1)}, u32[]{:S(2)}) copy-start(bf16[1,1,256,128]{3,2,1,0:T(8,128)(2,1)} %param.43) | copy-start | bytes 196612
  9.6 14.8 %copy-start.21 = (s32[1,1,8,8]{3,2,1,0:T(8,128)S(1)}, s32[1,1,8,8]{3,2,1,0:T(8,128)}, u32[]{:S(2)}) copy-start(s32[1,1,8,8]{3,2,1,0:T(8,128)} %param.28) | copy-start | bytes 772
  9.7 14.9 %copy-start.22 = (s32[1,1,8,16]{3,2,1,0:T(8,128)S(1)}, s32[1,1,8,16]{3,2,1,0:T(8,128)}, u32[]{:S(2)}) copy-start(s32[1,1,8,16]{3,2,1,0:T(8,128)} %param.31) | copy-start | bytes 1540
  9.7 16.3 %copy-start.31 = (s32[1,1,256]{2,1,0:T(1,128)S(1)}, s32[1,1,256]{2,1,0:T(1,128)}, u32[]{:S(2)}) copy-start(s32[1,1,256]{2,1,0:T(1,128)} %param.32) | copy-start | bytes 3076
  9.7 16.3 %copy-start.26 = (s32[1,1,2048]{2,1,0:T(1,128)S(1)}, s32[1,1,2048]{2,1,0:T(1,128)}, u32[]{:S(2)}) copy-start(s32[1,1,2048]{2,1,0:T(1,128)} %param.26) | copy-start | bytes 24580
  9.7 16.3 %copy-start.25 = (s32[1,1,2048]{2,1,0:T(1,128)S(1)}, s32[1,1,2048]{2,1,0:T(1,128)}, u32[]{:S(2)}) copy-start(s32[1,1,2048]{2,1,0:T(1,128)} %param.25) | copy-start | bytes 24580
  9.8 27.8 %copy-start.10 = (bf16[1,1,2048,128]{3,2,1,0:T(8,128)(2,1)S(1)}, bf16[1,1,2048,128]{3,2,1,0:T(8,128)(2,1)}, u32[]{:S(2)}) copy-start(bf16[1,1,2048,128]{3,2,1,0:T(8,128)(2,1)} %param.42) | copy-start | bytes 1572868
  9.8 28.0 %copy-start.11 = (bf16[1,1,2048,128]{3,2,1,0:T(8,128)(2,1)S(1)}, bf16[1,1,2048,128]{3,2,1,0:T(8,128)(2,1)}, u32[]{:S(2)}) copy-start(bf16[1,1,2048,128]{3,2,1,0:T(8,128)(2,1)} %param.24) | copy-start | bytes 1572868
  11.7 18.2 %collective-permute-start = (bf16[1,8,8,128]{3,2,0,1:T(8,128)(2,1)S(1)}, bf16[1,8,8,128]{3,2,0,1:T(8,128)(2,1)S(1)}, u32[]{:S(2)}, u32[]{:S(2)}) collective-permute-start(bf16[1,8,8,128]{3,2,0,1:T(8,128)(2,1)S(1)} %get-tuple-element.69), channel_id=1, source_target_pairs={{0,8},{8,16},{16,24},{24,32},{32,40},{40,48},{48,56},{56,64},{64,7... | collective-permute-start | bytes 49160 | tf_op jit(solution)/shard_map/ppermute | solution.py:19
  15.7 14.2 %collective-permute-start.1 = (bf16[1,8,8,128]{3,2,0,1:T(8,128)(2,1)S(1)}, bf16[1,8,8,128]{3,2,0,1:T(8,128)(2,1)S(1)}, u32[]{:S(2)}, u32[]{:S(2)}) collective-permute-start(bf16[1,8,8,128]{3,2,0,1:T(8,128)(2,1)S(1)} %get-tuple-element.70), channel_id=1, source_target_pairs={{8,0},{16,8},{24,16},{32,24},{40,32},{48,40},{56,48},{64,56},{72,6... | collective-permute-start | bytes 49160 | tf_op jit(solution)/shard_map/ppermute | solution.py:21
  19.2 11.4 %all-to-all-start.2 = ((bf16[8,16,128]{2,1,0:T(8,128)(2,1)}), bf16[8,16,128]{2,1,0:T(8,128)(2,1)S(1)}, u32[]{:S(2)}, u32[]{:S(2)}) async-start(bf16[8,16,128]{2,1,0:T(8,128)(2,1)} %bitcast.41), calls=%async_computation.2 | async-start | bytes 65536 | tf_op jit(solution)/shard_map/all_to_all | solution.py:194
  30.5 15.5 %all-to-all-start = ((bf16[3,8,8,128]{3,2,0,1:T(8,128)(2,1)}), bf16[3,8,8,128]{3,2,0,1:T(8,128)(2,1)S(1)}, u32[]{:S(2)}, u32[]{:S(2)}) async-start(bf16[3,8,8,128]{3,2,0,1:T(8,128)(2,1)} %pad_maximum_fusion.8), calls=%async_computation | async-start | bytes 98304 | tf_op jit(solution)/shard_map/all_to_all | solution.py:164
  37.8 51.7 %copy-start.2 = (bf16[1,1,2048,128]{2,3,1,0:T(8,128)(2,1)}, bf16[1,1,2048,128]{2,3,1,0:T(8,128)(2,1)S(1)}, u32[]{:S(2)}) copy-start(bf16[1,1,2048,128]{2,3,1,0:T(8,128)(2,1)S(1)} %copy.103) | copy-start | bytes 1572868
  38.0 17.1 %copy-start.7 = (bf16[1,1,2048,128]{2,3,1,0:T(8,128)(2,1)}, bf16[1,1,2048,128]{2,3,1,0:T(8,128)(2,1)S(1)}, u32[]{:S(2)}) copy-start(bf16[1,1,2048,128]{2,3,1,0:T(8,128)(2,1)S(1)} %copy.83) | copy-start | bytes 1572868
  46.7 8.4 %copy-start.36 = (f32[128]{0:T(128)S(1)}, f32[128]{0:T(128)}, u32[]{:S(2)}) copy-start(f32[128]{0:T(128)} %param.35) | copy-start | bytes 1540
  57.6 16.6 %copy-start.20 = (bf16[256,128]{1,0:T(8,128)(2,1)S(1)}, bf16[256,128]{1,0:T(8,128)(2,1)}, u32[]{:S(2)}) copy-start(bf16[256,128]{1,0:T(8,128)(2,1)} %param.38) | copy-start | bytes 196612
  57.6 16.6 %copy-start.37 = (f32[128]{0:T(128)S(1)}, f32[128]{0:T(128)}, u32[]{:S(2)}) copy-start(f32[128]{0:T(128)} %param.39) | copy-start | bytes 1540
  57.7 16.9 %copy-start.27 = (bf16[128,128]{1,0:T(8,128)(2,1)S(1)}, bf16[128,128]{1,0:T(8,128)(2,1)}, u32[]{:S(2)}) copy-start(bf16[128,128]{1,0:T(8,128)(2,1)} %param.40) | copy-start | bytes 98308
  59.9 15.0 %copy-start.35 = (f32[128]{0:T(128)S(1)}, f32[128]{0:T(128)}, u32[]{:S(2)}) copy-start(f32[128]{0:T(128)} %param.41) | copy-start | bytes 1540
  61.2 15.3 %copy-start.28 = (bf16[128,128]{1,0:T(8,128)(2,1)S(1)}, bf16[128,128]{1,0:T(8,128)(2,1)}, u32[]{:S(2)}) copy-start(bf16[128,128]{1,0:T(8,128)(2,1)} %param.40) | copy-start | bytes 98308
  94.1 21.2 %copy-start.34 = (f32[128]{0:T(128)S(1)}, f32[128]{0:T(128)}, u32[]{:S(2)}) copy-start(f32[128]{0:T(128)} %get-tuple-element.49) | copy-start | bytes 1540
  110.5 116.9 %all-to-all-start.1 = ((bf16[8,16,128]{2,1,0:T(8,128)(2,1)}), bf16[8,16,128]{2,1,0:T(8,128)(2,1)}, u32[]{:S(2)}, u32[]{:S(2)}) async-start(bf16[8,16,128]{2,1,0:T(8,128)(2,1)} %broadcast_select_fusion.2), calls=%async_computation.1 | async-start | bytes 65536 | tf_op jit(solution)/shard_map/all_to_all | solution.py:178
  115.3 361.0 %all-reduce.4.cloned.1.call-start = ((), (), s32[]{:S(2)}) async-start(), calls=%async_computation.4 | async-start | bytes 917504 | tf_op jit(solution)/shard_map/psum | solution.py:218
  210.5 29.6 %copy-start.16 = (bf16[256,128]{1,0:T(8,128)(2,1)S(1)}, bf16[256,128]{1,0:T(8,128)(2,1)}, u32[]{:S(2)}) copy-start(bf16[256,128]{1,0:T(8,128)(2,1)} %gather_fusion.4) | copy-start | bytes 196612
  210.5 29.6 %copy-start.32 = (pred[256]{0:T(512)(128)(4,1)S(1)}, pred[256]{0:T(512)(128)(4,1)}, u32[]{:S(2)}) copy-start(pred[256]{0:T(512)(128)(4,1)} %get-tuple-element.91) | copy-start | bytes 772
  210.5 29.6 %copy-start.33 = (pred[256]{0:T(512)(128)(4,1)S(1)}, pred[256]{0:T(512)(128)(4,1)}, u32[]{:S(2)}) copy-start(pred[256]{0:T(512)(128)(4,1)} %get-tuple-element.92) | copy-start | bytes 772
  225.3 15.7 %copy-start.18 = (f32[512,128]{1,0:T(8,128)S(1)}, f32[512,128]{1,0:T(8,128)}, u32[]{:S(2)}) copy-start(f32[512,128]{1,0:T(8,128)} %scatter_custom_fusion.5) | copy-start | bytes 786436
  227.4 9.1 %all-to-all-start.3 = ((bf16[3,8,8,128]{3,2,0,1:T(8,128)(2,1)}), bf16[3,8,8,128]{3,2,0,1:T(8,128)(2,1)S(1)}, u32[]{:S(2)}, u32[]{:S(2)}) async-start(bf16[3,8,8,128]{3,2,0,1:T(8,128)(2,1)} %copy.105), calls=%async_computation.3 | async-start | bytes 98304 | tf_op jit(solution)/shard_map/all_to_all | solution.py:205
  236.5 5.6 %collective-permute-start.2 = (bf16[1,8,8,128]{3,2,1,0:T(8,128)(2,1)S(1)}, bf16[1,8,8,128]{3,2,1,0:T(8,128)(2,1)S(1)}, u32[]{:S(2)}, u32[]{:S(2)}) collective-permute-start(bf16[1,8,8,128]{3,2,1,0:T(8,128)(2,1)S(1)} %get-tuple-element.67), channel_id=1, source_target_pairs={{0,8},{8,16},{16,24},{24,32},{32,40},{40,48},{48,56},{56,64},{64,7... | collective-permute-start | bytes 49160 | tf_op jit(solution)/shard_map/ppermute | solution.py:19
  238.8 4.9 collective-permute-start.3
  246.0 236.5 %copy-start.19 = (f32[512,128]{1,0:T(8,128)}, f32[512,128]{1,0:T(8,128)S(1)}, u32[]{:S(2)}) copy-start(f32[512,128]{1,0:T(8,128)S(1)} %scatter_custom_fusion.8) | copy-start | bytes 786436
  (16 other events, 30.2 us)
Sparse Core Ops, SparseCore 0:
  227.5 248.8 all-reduce.3
where the time goes:
time: 491 us; the launch traced here: 489 us
  waiting for transfers between devices  235 us (48%)
  blocking collectives  81.9 us (17%)
  other arithmetic  72.4 us (15%)
  local copies, waits for them, and re-layouts  46.6 us (9%)
  starting transfers between devices  28.1 us (6%)
  between operations  15.5 us (3%)
  matrix products  10.2 us (2%)
    psum x1, waiting for transfers between devices, per_device(): lax.psum((grads[0], grads[1], grads[2], grads[3], grads[4], grads[5], gra...  230 us
    psum x1, blocking collectives, per_device(): lax.psum((grads[0], grads[1], grads[2], grads[3], grads[4], grads[5], gra...  81.9 us
    scatter-add x1, other arithmetic, layer_backward(): jax.ops.segment_sum(d_edge_in[:, 2 * feature:], target_ids, num_segments=...  14.1 us
    scatter-add x1, other arithmetic, layer_forward(): jax.ops.segment_sum(message, target_ids, num_segments=cell_count, indices...  12.9 us
    scatter-add x1, other arithmetic, layer_backward(): jax.ops.segment_sum(d_edge_in[:, feature:2 * feature], source_ids, num_se...  12.2 us
  transfers between devices with their start and end apart: 9, of which 3 were waited for; matrix products, arithmetic and copies ran while one was open for 11% of the time, Pallas kernels for 0%

commit v1 on v0

v1 whole, which is shorter than its diff:
```python
import functools
import math

import jax
import jax.numpy as jnp
from jax import lax
from jax.experimental import pallas as pl
from jax.experimental.pallas import tpu as pltpu
from jax.sharding import Mesh
from jax.sharding import PartitionSpec as P

NORM_EPSILON = 1e-05
F32 = jnp.float32
BF16 = jnp.bfloat16
TILE = 256
VMEM_LIMIT = 56 * 1024 * 1024

ROWS_ONE = 48
ROWS_TWO = 176
GRAD_ROWS = 128


def mm(a, b):
    return lax.dot_general(a, b, (((1,), (0,)), ((), ())), preferred_element_type=F32)


def mm_nt(a, b):
    return lax.dot_general(a, b, (((1,), (1,)), ((), ())), preferred_element_type=F32)


def mm_tn(a, b):
    return lax.dot_general(a, b, (((0,), (0,)), ((), ())), preferred_element_type=F32)


def iota(shape, dim):
    return lax.broadcasted_iota(jnp.int32, shape, dim)


def onehot(mask):
    return jnp.where(mask, 1.0, 0.0).astype(BF16)


def two_parts(x):
    high = x.astype(BF16)
    low = (x - high.astype(F32)).astype(BF16)
    return high, low


def column_of(ids):
    a, b = ids.shape
    spread = jnp.broadcast_to(ids[:, None, :], (a, b, b))
    keep = iota((a, b, b), 1) == iota((a, b, b), 2)
    return jnp.sum(jnp.where(keep, spread, 0), axis=2, keepdims=True).reshape(a * b, 1)


def face_column(face_row, pick):
    spot = column_of(pick)
    shape = (spot.shape[0], face_row.shape[1])
    keep = spot == iota(shape, 1)
    return jnp.sum(jnp.where(keep, jnp.broadcast_to(face_row, shape), 0), axis=1, keepdims=True)


def onehot_rows(column, width):
    return onehot(column == iota((column.shape[0], width), 1))


def face_kernel(node_ref, bound_ref, pick_ref, down_ref, up_ref):
    node = node_ref[...]
    for k, out_ref in ((0, down_ref), (1, up_ref)):
        column = face_column(bound_ref[k : k + 1, :], pick_ref[k])
        out_ref[...] = mm(onehot_rows(column, node.shape[0]), node).astype(BF16)


def send_kernel(node_ref, intra_ref, second_ref, coarse_cot_ref, below_ref, above_ref, out_ref):
    node = node_ref[...]
    cells, feature = node.shape
    peers, halo = intra_ref.shape
    coarse = coarse_cot_ref.shape[0]
    intra = mm(onehot_rows(column_of(intra_ref[...]), cells), node)
    half = 0.5 * coarse_cot_ref[...].astype(F32)
    pool_rows = 16 * peers
    pool = mm(onehot(second_ref[...] - cells == iota((pool_rows, coarse), 0)), half.astype(BF16))
    parts = [
        intra.reshape(peers, halo, feature),
        below_ref[...].astype(F32).reshape(peers, halo, feature),
        above_ref[...].astype(F32).reshape(peers, halo, feature),
        jnp.zeros((peers, halo, feature), F32),
        pool.reshape(peers, 16, feature),
    ]
    out_ref[...] = jnp.concatenate(parts, axis=1).astype(BF16)


def silu_parts(pre):
    sig = 0.5 * jnp.tanh(0.5 * pre) + 0.5
    act = (pre * sig).astype(BF16)
    slope = sig * (1.0 + pre * (1.0 - sig))
    return act, slope


def norm_forward(out):
    centred = out - jnp.mean(out, axis=1, keepdims=True)
    inv = lax.rsqrt(jnp.mean(centred * centred, axis=1, keepdims=True) + NORM_EPSILON)
    return centred * inv, inv


def norm_backward(u, normed, inv, gain):
    scaled = u * gain
    inner = (
        scaled
        - jnp.mean(scaled, axis=1, keepdims=True)
        - normed * jnp.mean(scaled * normed, axis=1, keepdims=True)
    )
    return inner * inv


def fold_rows(x):
    rows, feature = x.shape
    return jnp.sum(x.reshape(rows // 8, 8, feature), axis=0)


def main_kernel(
    count_ref, src_ref, dst_ref, node_ref, recv_ref, edges_ref, cot_ref, coarse_cot_ref,
    first_ref, second_ref, match_ref, ew1_ref, eb1_ref, ew2_ref, eg_ref,
    nw1_ref, nb1_ref, nw2_ref, ng_ref,
    new_edges_ref, d_edges_ref, d_node_ref, fresh_ref, send_ref,
    table_ref, t2_ref, ohd_ref, oht_ref, agg_ref, act_ref, slope_ref, normed_ref, inv_ref,
    dagg_ref, s_ref, dw1_ref, dw2_ref, db1_ref, dg_ref, grads_ref,
):
    cells, feature = node_ref.shape
    slots = edges_ref.shape[0]
    peers = recv_ref.shape[0]
    tiles = slots // TILE
    count = count_ref[0, 0]
    node = node_ref[...]
    received = recv_ref[...].astype(F32)
    halo_rows = 3 * 8 * peers
    wide = table_ref.shape[0]
    table_ref[0:cells, :] = node
    halo = jnp.concatenate(
        [received[:, 8 * k : 8 * k + 8, :].reshape(8 * peers, feature) for k in range(3)]
        + [jnp.zeros((wide - cells - halo_rows, feature), F32)],
        axis=0,
    )
    table_ref[cells:wide, :] = halo.astype(BF16)
    ew1_edge = ew1_ref[0:feature, :]
    ew1_src = ew1_ref[feature : 2 * feature, :]
    ew1_dst = ew1_ref[2 * feature : 3 * feature, :]
    high, low = two_parts(mm(table_ref[...], ew1_src))
    t2_ref[0:wide, 0:feature] = high
    t2_ref[0:wide, feature:] = low
    high, low = two_parts(mm(node, ew1_dst) + eb1_ref[...])
    t2_ref[wide:, 0:feature] = high
    t2_ref[wide:, feature:] = low
    agg_ref[...] = jnp.zeros_like(agg_ref)
    ew2 = ew2_ref[...]
    eg = eg_ref[...]

    def live_of(start):
        return iota((TILE, feature), 0) + start < count

    def forward_tile(i, carry):
        start = pl.multiple_of(i * TILE, TILE)
        rows = pl.ds(start, TILE)
        src = src_ref[:, rows]
        dst = dst_ref[:, rows]
        src_col = jnp.broadcast_to(src, (128, TILE)).T
        dst_col = jnp.broadcast_to(dst, (128, TILE)).T
        lane = iota((TILE, 128), 1)
        hot_src = jnp.concatenate(
            [onehot(src_col == lane + 128 * k) for k in range(wide // 128)], axis=1
        )
        hot_dst = jnp.concatenate(
            [onehot(dst_col == lane + 128 * k) for k in range(cells // 128)], axis=1
        )
        ohd_ref[rows, :] = hot_dst
        both = mm(hot_src, t2_ref[0:wide, :]) + mm(hot_dst, t2_ref[wide:, :])
        edges = edges_ref[rows, :]
        pre = both[:, 0:feature] + both[:, feature:] + mm(edges, ew1_edge)
        act, slope = silu_parts(pre)
        act_ref[rows, :] = act
        slope_ref[rows, :] = slope
        normed, inv = norm_forward(mm(act, ew2))
        normed_ref[rows, :] = normed
        inv_ref[rows, :] = inv
        live = live_of(start)
        message = jnp.where(live, normed * eg, 0.0)
        new_edges_ref[rows, :] = jnp.where(live, edges.astype(F32) + message, 0.0).astype(BF16)
        hot = onehot(dst == iota((cells, TILE), 0))
        oht_ref[:, rows] = hot
        agg_ref[...] += mm(hot, jnp.concatenate(two_parts(message), axis=1))
        return carry

    lax.fori_loop(0, tiles, forward_tile, 0)

    aggregate = (agg_ref[:, 0:feature] + agg_ref[:, feature:]).astype(BF16)
    nw1_node = nw1_ref[0:feature, :]
    nw1_agg = nw1_ref[feature:, :]
    pre = mm(node, nw1_node) + mm(aggregate, nw1_agg) + nb1_ref[...]
    act, slope = silu_parts(pre)
    nw2 = nw2_ref[...]
    ng = ng_ref[...]
    normed, inv = norm_forward(mm(act, nw2))
    fresh = (node.astype(F32) + normed * ng).astype(BF16)
    fresh_ref[...] = fresh

    coarse = coarse_cot_ref.shape[0]
    half = (0.5 * coarse_cot_ref[...].astype(F32)).astype(BF16)
    cell_row = iota((cells, coarse), 0)
    pooled = onehot((first_ref[...] == cell_row) | (second_ref[...] == cell_row))
    returned = recv_ref[:, ROWS_ONE - 16 : ROWS_ONE, :].reshape(16 * peers, feature)
    hot_match = onehot_rows(column_of(match_ref[...]), cells)
    d_fresh = mm(pooled, half) + mm_tn(hot_match, returned)
    match_rows = mm(hot_match, fresh)

    d_out = norm_backward(d_fresh, normed, inv, ng)
    grads_ref[899:900, :] = jnp.sum(d_fresh * normed, axis=0, keepdims=True)
    d_out_half = d_out.astype(BF16)
    grads_ref[768:896, :] = mm_tn(act, d_out_half)
    d_pre = mm_nt(d_out_half, nw2) * slope
    grads_ref[898:899, :] = jnp.sum(d_pre, axis=0, keepdims=True)
    d_pre_half = d_pre.astype(BF16)
    grads_ref[512:640, :] = mm_tn(node, d_pre_half)
    grads_ref[640:768, :] = mm_tn(aggregate, d_pre_half)
    d_node_ref[...] = d_fresh + mm_nt(d_pre_half, nw1_node)
    high, low = two_parts(mm_nt(d_pre_half, nw1_agg))
    dagg_ref[:, 0:feature] = high
    dagg_ref[:, feature:] = low

    s_ref[...] = jnp.zeros_like(s_ref)
    dw1_ref[...] = jnp.zeros_like(dw1_ref)
    dw2_ref[...] = jnp.zeros_like(dw2_ref)
    db1_ref[...] = jnp.zeros_like(db1_ref)
    dg_ref[...] = jnp.zeros_like(dg_ref)

    def backward_tile(i, carry):
        start = pl.multiple_of(i * TILE, TILE)
        rows = pl.ds(start, TILE)
        both = mm(ohd_ref[rows, :], dagg_ref[...])
        live = live_of(start)
        cot = jnp.where(live, cot_ref[rows, :].astype(F32), 0.0)
        u = jnp.where(live, cot + (both[:, 0:feature] + both[:, feature:]), 0.0)
        normed = normed_ref[rows, :]
        d_out_half = norm_backward(u, normed, inv_ref[rows, :], eg).astype(BF16)
        dg_ref[...] += fold_rows(u * normed)
        dw2_ref[...] += mm_tn(act_ref[rows, :], d_out_half)
        d_pre = mm_nt(d_out_half, ew2) * slope_ref[rows, :]
        db1_ref[...] += fold_rows(d_pre)
        d_pre_half = d_pre.astype(BF16)
        d_edges_ref[rows, :] = (cot + mm_nt(d_pre_half, ew1_edge)).astype(BF16)
        dw1_ref[...] += mm_tn(edges_ref[rows, :], d_pre_half)
        hot = onehot(src_ref[:, rows] == iota((wide, TILE), 0))
        s_ref[0:wide, :] += mm(hot, d_pre_half)
        s_ref[wide:, :] += mm(oht_ref[:, rows], d_pre_half)
        return carry

    lax.fori_loop(0, tiles, backward_tile, 0)

    grads_ref[0:128, :] = dw1_ref[...]
    grads_ref[384:512, :] = dw2_ref[...]
    grads_ref[896:897, :] = jnp.sum(db1_ref[...], axis=0, keepdims=True)
    grads_ref[897:898, :] = jnp.sum(dg_ref[...], axis=0, keepdims=True)
    grads_ref[900:, :] = jnp.zeros_like(grads_ref[900:, :])
    high, low = two_parts(s_ref[0:wide, :])
    table = table_ref[...]
    grads_ref[128:256, :] = mm_tn(table, high) + mm_tn(table, low)
    d_table = mm_nt(high, ew1_src) + mm_nt(low, ew1_src)
    high, low = two_parts(s_ref[wide:, :])
    grads_ref[256:384, :] = mm_tn(node, high) + mm_tn(node, low)
    d_node_ref[...] += d_table[0:cells, :] + (mm_nt(high, ew1_dst) + mm_nt(low, ew1_dst))
    kinds = [
        d_table[cells + 8 * peers * k : cells + 8 * peers * (k + 1), :].reshape(peers, 8, feature)
        for k in range(3)
    ]
    parts = kinds + [
        jnp.zeros((peers, 8, feature), F32),
        match_rows.reshape(peers, 16, feature),
        grads_ref[...].reshape(peers, GRAD_ROWS, feature),
    ]
    send_ref[...] = jnp.concatenate(parts, axis=1).astype(BF16)


def split_kernel(recv_ref, down_ref, up_ref, sum_ref):
    peers, _, feature = recv_ref.shape
    head = recv_ref[:, 0:32, :].astype(F32)
    down_ref[...] = head[:, 8:16, :].reshape(8 * peers, feature).astype(BF16)
    up_ref[...] = head[:, 16:24, :].reshape(8 * peers, feature).astype(BF16)
    total = recv_ref[0, 48:, :].astype(F32)
    for p in range(1, peers):
        total = total + recv_ref[p, 48:, :].astype(F32)
    total = total.astype(BF16)
    for p in range(sum_ref.shape[0]):
        sum_ref[p] = total


def add_kernel(scale, recv_ref, out_ref):
    total = recv_ref[0].astype(F32)
    for p in range(1, recv_ref.shape[0]):
        total = total + recv_ref[p].astype(F32)
    total = (total * scale).astype(BF16)
    for p in range(out_ref.shape[0]):
        out_ref[p] = total


def finish_kernel(
    recv_ref, from_above_ref, from_below_ref, d_node_ref, fresh_ref, intra_ref, bound_ref,
    pick_ref, first_ref, second_ref, d_out_ref, coarse_ref,
):
    peers, _, feature = recv_ref.shape
    cells = d_node_ref.shape[0]
    head = recv_ref[:, 0:16, :].astype(F32)
    own = head[:, 0:8, :].reshape(8 * peers, feature).astype(BF16)
    hot = onehot_rows(column_of(intra_ref[...]), cells)
    total = mm_tn(hot, own)
    for k, back_ref in ((0, from_below_ref), (1, from_above_ref)):
        column = face_column(bound_ref[k : k + 1, :], pick_ref[k])
        total = total + mm_tn(onehot_rows(column, cells), back_ref[...])
    d_out_ref[...] = d_node_ref[...] + total
    partners = recv_ref[:, 32:48, :].reshape(16 * peers, feature)
    coarse = coarse_ref.shape[0]
    cell_row = iota((cells, coarse), 0)
    near = onehot((first_ref[...] == cell_row) | (second_ref[...] == cell_row))
    far = onehot(second_ref[...] - cells == iota((16 * peers, coarse), 0))
    coarse_ref[...] = (0.5 * (mm_tn(near, fresh_ref[...]) + mm_tn(far, partners))).astype(BF16)


def unpack_kernel(recv_ref, w1_ref, w2_ref, nw1_ref, nw2_ref, b1_ref, g_ref, nb1_ref, ng_ref):
    for p in range(3):
        w1_ref[128 * p : 128 * p + 128, :] = recv_ref[p].astype(F32)
    w2_ref[...] = recv_ref[3].astype(F32)
    nw1_ref[0:128, :] = recv_ref[4].astype(F32)
    nw1_ref[128:256, :] = recv_ref[5].astype(F32)
    nw2_ref[...] = recv_ref[6].astype(F32)
    tail = recv_ref[7, 0:16, :].astype(F32)
    b1_ref[...] = tail[0:1, :]
    g_ref[...] = tail[1:2, :]
    nb1_ref[...] = tail[2:3, :]
    ng_ref[...] = tail[3:4, :]


def call(kernel, out_shape, *args, scratch=(), smem=(), name=None, cost=None):
    specs = [
        pl.BlockSpec(memory_space=pltpu.SMEM if i in smem else pltpu.VMEM) for i in range(len(args))
    ]
    return pl.pallas_call(
        kernel,
        out_shape=out_shape,
        in_specs=specs,
        out_specs=jax.tree.map(lambda _: pl.BlockSpec(memory_space=pltpu.VMEM), out_shape),
        scratch_shapes=list(scratch),
        compiler_params=pltpu.CompilerParams(vmem_limit_bytes=VMEM_LIMIT),
        name=name,
        cost_estimate=cost,
    )(*args)


def shape_of(shape, dtype):
    return jax.ShapeDtypeStruct(shape, dtype)


def per_device(
    slabs, node, edges, edge_src, edge_dst, edge_count, intra_idx, bound_idx, cross_pick,
    match_send, pool_first, pool_second, edge_w1, edge_b1, edge_w2, edge_gain,
    node_w1, node_b1, node_w2, node_gain, edge_cot, coarse_cot,
):
    node, edges, edge_cot, coarse_cot = node[0, 0], edges[0, 0], edge_cot[0, 0], coarse_cot[0, 0]
    intra, bound, pick, match = intra_idx[0, 0], bound_idx[0, 0], cross_pick[0], match_send[0, 0]
    first, second = pool_first[0], pool_second[0]
    src, dst = edge_src[0], edge_dst[0]
    cells, feature = node.shape
    slots = edges.shape[0]
    coarse = coarse_cot.shape[0]
    peers = lax.axis_size("sub")
    planes, columns = lax.axis_size("z"), lax.axis_size("y")
    dom = ("z", "y")
    upward = [(i, i + 1) for i in range(slabs - 1)]
    downward = [(i + 1, i) for i in range(slabs - 1)]
    face = shape_of((8 * peers, feature), BF16)
    wide = -(-(cells + 24 * peers) // 256) * 256

    to_down, to_up = call(face_kernel, (face, face), node, bound, pick, name="faces")
    from_below = lax.ppermute(to_up, dom, upward)
    from_above = lax.ppermute(to_down, dom, downward)
    sent = call(
        send_kernel, shape_of((peers, ROWS_ONE, feature), BF16),
        node, intra, second, coarse_cot, from_below, from_above, name="send",
    )
    received = lax.all_to_all(sent, "sub", split_axis=0, concat_axis=0, tiled=True)

    new_edges, d_edges, d_node, fresh, sent = call(
        main_kernel,
        (
            shape_of((slots, feature), BF16),
            shape_of((slots, feature), BF16),
            shape_of((cells, feature), F32),
            shape_of((cells, feature), BF16),
            shape_of((peers, ROWS_TWO, feature), BF16),
        ),
        edge_count, src, dst, node, received, edges, edge_cot, coarse_cot, first, second, match,
        edge_w1, edge_b1[None], edge_w2, edge_gain[None],
        node_w1, node_b1[None], node_w2, node_gain[None],
        smem=(0,),
        scratch=(
            pltpu.VMEM((wide, feature), BF16),
            pltpu.VMEM((wide + cells, 2 * feature), BF16),
            pltpu.VMEM((slots, cells), BF16),
            pltpu.VMEM((cells, slots), BF16),
            pltpu.VMEM((cells, 2 * feature), F32),
            pltpu.VMEM((slots, feature), BF16),
            pltpu.VMEM((slots, feature), F32),
            pltpu.VMEM((slots, feature), F32),
            pltpu.VMEM((slots, 1), F32),
            pltpu.VMEM((cells, 2 * feature), BF16),
            pltpu.VMEM((wide + cells, feature), F32),
            pltpu.VMEM((feature, feature), F32),
            pltpu.VMEM((feature, feature), F32),
            pltpu.VMEM((8, feature), F32),
            pltpu.VMEM((8, feature), F32),
            pltpu.VMEM((peers * GRAD_ROWS, feature), F32),
        ),
        name="layer",
    )
    received = lax.all_to_all(sent, "sub", split_axis=0, concat_axis=0, tiled=True)
    piece = (GRAD_ROWS, feature)
    back_down, back_up, partial = call(
        split_kernel, (face, face, shape_of((planes,) + piece, BF16)), received, name="split"
    )
    from_above = lax.ppermute(back_down, dom, downward)
    from_below = lax.ppermute(back_up, dom, upward)
    partial = lax.all_to_all(partial, "z", split_axis=0, concat_axis=0, tiled=True)
    d_node, coarse_out = call(
        finish_kernel,
        (shape_of((cells, feature), F32), shape_of((coarse, feature), BF16)),
        received, from_above, from_below, d_node, fresh, intra, bound, pick, first, second,
        name="finish",
        cost=pl.CostEstimate(flops=300_000_000, bytes_accessed=2_000_000, transcendentals=0),
    )
    partial = call(
        functools.partial(add_kernel, 1.0), shape_of((columns,) + piece, BF16), partial, name="add_z"
    )
    partial = lax.all_to_all(partial, "y", split_axis=0, concat_axis=0, tiled=True)
    scale = 1.0 / math.sqrt(slabs * peers * slots)
    partial = call(
        functools.partial(add_kernel, scale), shape_of((peers,) + piece, BF16), partial, name="add_y"
    )
    grads = lax.all_to_all(partial, "sub", split_axis=0, concat_axis=0, tiled=True)
    row = shape_of((1, feature), F32)
    w1, w2, nw1, nw2, b1, g, nb1, ng = call(
        unpack_kernel,
        (
            shape_of((3 * feature, feature), F32),
            shape_of((feature, feature), F32),
            shape_of((2 * feature, feature), F32),
            shape_of((feature, feature), F32),
            row, row, row, row,
        ),
        grads,
        name="unpack",
    )
    return (
        new_edges[None, None], coarse_out[None, None], d_node[None, None], d_edges[None, None],
        w1, b1[0], w2, g[0], nw1, nb1[0], nw2, ng[0],
    )


def solution(mesh):
    slabs, peers = mesh.shape["dom"], mesh.shape["sub"]
    columns = 4 if slabs % 8 == 0 else 2
    inner = Mesh(mesh.devices.reshape(slabs // columns, columns, peers), ("z", "y", "sub"))
    dom = ("z", "y")
    four, three = P(dom, "sub", None, None), P(dom, "sub", None)
    return jax.shard_map(
        functools.partial(per_device, slabs),
        mesh=inner,
        in_specs=(
            four, four, three, three, P(dom, "sub"), four, four, P("sub", None, None, None),
            four, three, three, P(), P(), P(), P(), P(), P(), P(), P(), four, four,
        ),
        out_specs=(four, four, four, four) + (P(),) * 8,
        check_vma=False,
    )
```

time: 491 us -> 116 us (0.24)
  the two profiles are of different devices: /device:TPU:1 before, /device:TPU:34 now
where the time goes in v1:
time: 116 us; the launch traced here: 115 us
  blocking collectives  43.7 us (38%)
  Pallas kernels  33.1 us (29%)
  starting transfers between devices  23.6 us (20%)
  waiting for transfers between devices  11.1 us (10%)
  local copies, waits for them, and re-layouts  2.56 us (2%)
  between operations  1.38 us (1%)
    pallas_call x8, Pallas kernels, call(): pl.pallas_call(kernel, out_shape=out_shape, in_specs=specs, out_specs=jax...  33.1 us
    all_to_all x1, blocking collectives, per_device(): lax.all_to_all(partial, 'z', split_axis=0, concat_axis=0, tiled=True)  20.1 us
    all_to_all x1, blocking collectives, per_device(): lax.all_to_all(sent, 'sub', split_axis=0, concat_axis=0, tiled=True)  12.7 us
    all_to_all x1, blocking collectives, per_device(): lax.all_to_all(partial, 'y', split_axis=0, concat_axis=0, tiled=True)  10.9 us
    ppermute x1, waiting for transfers between devices, per_device(): from_below = lax.ppermute(back_up, dom, upward)  5.79 us
    all_to_all x1, starting transfers between devices, per_device(): lax.all_to_all(partial, 'sub', split_axis=0, concat_axis=0, tiled=True)  4.91 us
    all_to_all x1, starting transfers between devices, per_device(): lax.all_to_all(sent, 'sub', split_axis=0, concat_axis=0, tiled=True)  4.83 us
    ppermute x1, starting transfers between devices, per_device(): from_above = lax.ppermute(to_down, dom, downward)  4.47 us
  transfers between devices with their start and end apart: 6, of which 3 were waited for; matrix products, arithmetic and copies ran while one was open for 0% of the time, Pallas kernels for 2%

profile of v1, /device:TPU:34, one launch (start us, length us, event | category | flops | bytes accessed | tf_op | source)
XLA Modules:
  0.0 115.3 jit_solution(6958525401002797606)
XLA Ops:
  0.6 1.9 %faces.1 = (bf16[64,128]{1,0:T(8,128)(2,1)}, bf16[64,128]{1,0:T(8,128)(2,1)}) custom-call(bf16[512,128]{1,0:T(8,128)(2,1)} %bitcast.24, s32[2,16]{1,0:T(2,128)} %bitcast.41, s32[2,8,8]{2,1,0:T(8,128)} %bitcast.33), custom_call_target="tpu_custom_call" | custom-call | tf_op jit(solution)/shard_map/faces/pallas_call | solution.py:344
  2.5 3.5 %collective-permute-start = (bf16[64,128]{1,0:T(8,128)(2,1)}, bf16[64,128]{1,0:T(8,128)(2,1)S(1)}, u32[]{:S(2)}, u32[]{:S(2)}) collective-permute-start(bf16[64,128]{1,0:T(8,128)(2,1)} %get-tuple-element.32), channel_id=1, source_target_pairs={{0,8},{8,16},{16,24},{24,32},{32,40},{40,48},{48,56},{56,64},{64,7... | collective-permute-start | bytes 49160 | tf_op jit(solution)/shard_map/ppermute | solution.py:381
  6.0 4.5 %collective-permute-start.1 = (bf16[64,128]{1,0:T(8,128)(2,1)}, bf16[64,128]{1,0:T(8,128)(2,1)S(1)}, u32[]{:S(2)}, u32[]{:S(2)}) collective-permute-start(bf16[64,128]{1,0:T(8,128)(2,1)} %get-tuple-element.33), channel_id=1, source_target_pairs={{8,0},{16,8},{24,16},{32,24},{40,32},{48,40},{56,48},{64,56},{72,6... | collective-permute-start | bytes 49160 | tf_op jit(solution)/shard_map/ppermute | solution.py:382
  10.5 0.0 collective-permute-done.below_ref
  10.5 0.0 copy-start.2
  10.5 1.6 %collective-permute-done.1.above_ref = bf16[64,128]{1,0:T(8,128)(2,1)S(1)} collective-permute-done((bf16[64,128]{1,0:T(8,128)(2,1)}, bf16[64,128]{1,0:T(8,128)(2,1)S(1)}, u32[]{:S(2)}, u32[]{:S(2)}) %collective-permute-start.1) | collective-permute-done | bytes 16416 | tf_op jit(solution)/shard_map/ppermute | solution.py:382
  12.1 0.0 copy-done.2
  12.1 0.6 copy-done.3
  12.7 1.8 %send.1 = bf16[8,48,128]{2,1,0:T(8,128)(2,1)} custom-call(bf16[512,128]{1,0:T(8,128)(2,1)} %bitcast.25, s32[8,8]{1,0:T(8,128)} %bitcast.36, s32[1,256]{1,0:T(1,128)} %bitcast.38, bf16[256,128]{1,0:T(8,128)(2,1)} %bitcast.29, bf16[64,128]{1,0:T(8,128)(2,1)} %copy-done.2, bf16[64,128]{1,0:T(8,128)(2,1)} %copy-done.3), custom_call_target="tpu_custom_call" | custom-call | tf_op jit(solution)/shard_map/send/pallas_call | solution.py:344
  14.5 4.8 %all-to-all-start = ((bf16[8,48,128]{2,1,0:T(8,128)(2,1)}), bf16[8,48,128]{2,1,0:T(8,128)(2,1)S(1)}, u32[]{:S(2)}, u32[]{:S(2)}) async-start(bf16[8,48,128]{2,1,0:T(8,128)(2,1)} %send.1), calls=%async_computation | async-start | bytes 196608 | tf_op jit(solution)/shard_map/all_to_all | solution.py:387
  20.0 3.7 %all-to-all-done.recv_ref = bf16[8,48,128]{2,1,0:T(8,128)(2,1)S(1)} async-done(((bf16[8,48,128]{2,1,0:T(8,128)(2,1)}), bf16[8,48,128]{2,1,0:T(8,128)(2,1)S(1)}, u32[]{:S(2)}, u32[]{:S(2)}) %all-to-all-start) | async-done | bytes 98336 | tf_op jit(solution)/shard_map/all_to_all | solution.py:387
  23.7 0.6 copy-done.1
  24.4 19.9 %layer.1 = (bf16[2048,128]{1,0:T(8,128)(2,1)}, bf16[2048,128]{1,0:T(8,128)(2,1)}, f32[512,128]{1,0:T(8,128)}, bf16[512,128]{1,0:T(8,128)(2,1)}, bf16[8,176,128]{2,1,0:T(8,128)(2,1)}) custom-call(s32[1,1]{1,0:T(1,128)S(6)} %copy.33.count_ref, s32[1,2048]{1,0:T(1,128)} %bitcast.31, s32[1,2048]{1,0:T(1,128)} %bitcast.32, bf16[512,128]{1,0:T(8,128)(2,1)} %bitcast.26, ...), custom_call_target="tpu_custom_call" | custom-call | tf_op jit(solution)/shard_map/layer/pallas_call | solution.py:344
  44.3 12.7 %all_to_all.25.recv_ref = bf16[8,176,128]{2,1,0:T(8,128)(2,1)} all-to-all(bf16[8,176,128]{2,1,0:T(8,128)(2,1)} %get-tuple-element.35), channel_id=1, replica_groups=mesh['z'=8,'y'=4,'sub'=8] {'sub'}, dimensions={0} | all-to-all | bytes 720896 | tf_op jit(solution)/shard_map/all_to_all | solution.py:422
  57.0 1.7 %split.1 = (bf16[64,128]{1,0:T(8,128)(2,1)}, bf16[64,128]{1,0:T(8,128)(2,1)}, bf16[8,128,128]{2,1,0:T(8,128)(2,1)}) custom-call(bf16[8,176,128]{2,1,0:T(8,128)(2,1)} %all_to_all.25.recv_ref), custom_call_target="tpu_custom_call" | custom-call | tf_op jit(solution)/shard_map/split/pallas_call | solution.py:344
  58.7 20.1 %all_to_all.26.recv_ref = bf16[8,128,128]{2,1,0:T(8,128)(2,1)} all-to-all(bf16[8,128,128]{2,1,0:T(8,128)(2,1)} %get-tuple-element.43), channel_id=1, replica_groups=mesh['z'=8,'y'=4,'sub'=8] {'z'}, dimensions={0} | all-to-all | bytes 524288 | tf_op jit(solution)/shard_map/all_to_all | solution.py:429
  78.8 1.6 %add_z.1 = bf16[4,128,128]{2,1,0:T(8,128)(2,1)} custom-call(bf16[8,128,128]{2,1,0:T(8,128)(2,1)} %all_to_all.26.recv_ref), custom_call_target="tpu_custom_call" | custom-call | tf_op jit(solution)/shard_map/add_z/pallas_call | solution.py:344
  80.5 10.9 %all_to_all.27.recv_ref = bf16[4,128,128]{2,1,0:T(8,128)(2,1)} all-to-all(bf16[4,128,128]{2,1,0:T(8,128)(2,1)} %add_z.1), channel_id=1, replica_groups=mesh['z'=8,'y'=4,'sub'=8] {'y'}, dimensions={0} | all-to-all | bytes 262144 | tf_op jit(solution)/shard_map/all_to_all | solution.py:440
  91.3 1.6 %add_y.1 = bf16[8,128,128]{2,1,0:T(8,128)(2,1)} custom-call(bf16[4,128,128]{2,1,0:T(8,128)(2,1)} %all_to_all.27.recv_ref), custom_call_target="tpu_custom_call" | custom-call | tf_op jit(solution)/shard_map/add_y/pallas_call | solution.py:344
  93.0 4.9 %all-to-all-start.4 = ((bf16[8,128,128]{2,1,0:T(8,128)(2,1)}), bf16[8,128,128]{2,1,0:T(8,128)(2,1)S(1)}, u32[]{:S(2)}, u32[]{:S(2)}) async-start(bf16[8,128,128]{2,1,0:T(8,128)(2,1)} %add_y.1), calls=%async_computation.4 | async-start | bytes 524288 | tf_op jit(solution)/shard_map/all_to_all | solution.py:445
  97.9 0.0 copy-done.5
  97.9 4.0 %collective-permute-start.2 = (bf16[64,128]{1,0:T(8,128)(2,1)S(1)}, bf16[64,128]{1,0:T(8,128)(2,1)S(1)}, u32[]{:S(2)}, u32[]{:S(2)}) collective-permute-start(bf16[64,128]{1,0:T(8,128)(2,1)S(1)} %copy-done.5), channel_id=1, source_target_pairs={{8,0},{16,8},{24,16},{32,24},{40,32},{48,40},{56,48},{64,56},{72,6... | collective-permute-start | bytes 49160 | tf_op jit(solution)/shard_map/ppermute | solution.py:427
  101.9 0.0 copy-done.4
  101.9 1.9 %collective-permute-start.3 = (bf16[64,128]{1,0:T(8,128)(2,1)S(1)}, bf16[64,128]{1,0:T(8,128)(2,1)S(1)}, u32[]{:S(2)}, u32[]{:S(2)}) collective-permute-start(bf16[64,128]{1,0:T(8,128)(2,1)S(1)} %copy-done.4), channel_id=1, source_target_pairs={{0,8},{8,16},{16,24},{24,32},{32,40},{40,48},{48,56},{56,64},{64,7... | collective-permute-start | bytes 49160 | tf_op jit(solution)/shard_map/ppermute | solution.py:428
  103.8 0.0 collective-permute-done.2.from_above_ref
  103.8 0.0 copy-start.6
  103.8 5.8 %collective-permute-done.3.from_below_ref = bf16[64,128]{1,0:T(8,128)(2,1)S(1)} collective-permute-done((bf16[64,128]{1,0:T(8,128)(2,1)S(1)}, bf16[64,128]{1,0:T(8,128)(2,1)S(1)}, u32[]{:S(2)}, u32[]{:S(2)}) %collective-permute-start.3) | collective-permute-done | bytes 16416 | tf_op jit(solution)/shard_map/ppermute | solution.py:428
  109.6 0.6 copy-done.7
  110.2 2.7 %finish.1 = (f32[512,128]{1,0:T(8,128)}, bf16[256,128]{1,0:T(8,128)(2,1)}) custom-call(bf16[8,176,128]{2,1,0:T(8,128)(2,1)} %all_to_all.25.recv_ref, bf16[64,128]{1,0:T(8,128)(2,1)} %copy-done.6, bf16[64,128]{1,0:T(8,128)(2,1)} %copy-done.7, f32[512,128]{1,0:T(8,128)} %get-tuple-element.38.d_node_ref, bf16[512,128]{1,0:T(8,128)(2,1)} %get-tuple-element.39.fresh_ref, ...), custom_call_target="tpu_custom_call" | custom-call | flops 300000000 | bytes 2000000 | tf_op jit(solution)/shard_map/finish/pallas_call | solution.py:344
  112.9 0.0 all-to-all-done.4.recv_ref
  112.9 0.7 copy-done
  113.6 1.7 %unpack.1 = (f32[384,128]{1,0:T(8,128)}, f32[128,128]{1,0:T(8,128)}, f32[256,128]{1,0:T(8,128)}, f32[128,128]{1,0:T(8,128)}, f32[1,128]{1,0:T(1,128)}, /*index=5...) custom-call(bf16[8,128,128]{2,1,0:T(8,128)(2,1)} %copy-done), custom_call_target="tpu_custom_call" | custom-call | tf_op jit(solution)/shard_map/unpack/pallas_call | solution.py:344
  (7 shorter events, 0.0 us)
Async XLA Ops:
  2.5 8.0 %collective-permute-start = (bf16[64,128]{1,0:T(8,128)(2,1)}, bf16[64,128]{1,0:T(8,128)(2,1)S(1)}, u32[]{:S(2)}, u32[]{:S(2)}) collective-permute-start(bf16[64,128]{1,0:T(8,128)(2,1)} %get-tuple-element.32), channel_id=1, source_target_pairs={{0,8},{8,16},{16,24},{24,32},{32,40},{40,48},{48,56},{56,64},{64,7... | collective-permute-start | bytes 49160 | tf_op jit(solution)/shard_map/ppermute | solution.py:381
  6.0 6.1 %collective-permute-start.1 = (bf16[64,128]{1,0:T(8,128)(2,1)}, bf16[64,128]{1,0:T(8,128)(2,1)S(1)}, u32[]{:S(2)}, u32[]{:S(2)}) collective-permute-start(bf16[64,128]{1,0:T(8,128)(2,1)} %get-tuple-element.33), channel_id=1, source_target_pairs={{8,0},{16,8},{24,16},{32,24},{40,32},{48,40},{56,48},{64,56},{72,6... | collective-permute-start | bytes 49160 | tf_op jit(solution)/shard_map/ppermute | solution.py:382
  10.5 1.6 %copy-start.2 = (bf16[64,128]{1,0:T(8,128)(2,1)}, bf16[64,128]{1,0:T(8,128)(2,1)S(1)}, u32[]{:S(2)}) copy-start(bf16[64,128]{1,0:T(8,128)(2,1)S(1)} %collective-permute-done.below_ref) | copy-start | bytes 49156
  12.1 0.6 copy-start.3
  14.5 9.2 %all-to-all-start = ((bf16[8,48,128]{2,1,0:T(8,128)(2,1)}), bf16[8,48,128]{2,1,0:T(8,128)(2,1)S(1)}, u32[]{:S(2)}, u32[]{:S(2)}) async-start(bf16[8,48,128]{2,1,0:T(8,128)(2,1)} %send.1), calls=%async_computation | async-start | bytes 196608 | tf_op jit(solution)/shard_map/all_to_all | solution.py:387
  23.7 0.6 copy-start.1
  93.0 4.9 %copy-start.5 = (bf16[64,128]{1,0:T(8,128)(2,1)S(1)}, bf16[64,128]{1,0:T(8,128)(2,1)}, u32[]{:S(2)}) copy-start(bf16[64,128]{1,0:T(8,128)(2,1)} %get-tuple-element.36) | copy-start | bytes 49156
  93.0 8.9 %copy-start.4 = (bf16[64,128]{1,0:T(8,128)(2,1)S(1)}, bf16[64,128]{1,0:T(8,128)(2,1)}, u32[]{:S(2)}) copy-start(bf16[64,128]{1,0:T(8,128)(2,1)} %get-tuple-element.37) | copy-start | bytes 49156
  93.0 19.9 %all-to-all-start.4 = ((bf16[8,128,128]{2,1,0:T(8,128)(2,1)}), bf16[8,128,128]{2,1,0:T(8,128)(2,1)S(1)}, u32[]{:S(2)}, u32[]{:S(2)}) async-start(bf16[8,128,128]{2,1,0:T(8,128)(2,1)} %add_y.1), calls=%async_computation.4 | async-start | bytes 524288 | tf_op jit(solution)/shard_map/all_to_all | solution.py:445
  97.9 5.9 %collective-permute-start.2 = (bf16[64,128]{1,0:T(8,128)(2,1)S(1)}, bf16[64,128]{1,0:T(8,128)(2,1)S(1)}, u32[]{:S(2)}, u32[]{:S(2)}) collective-permute-start(bf16[64,128]{1,0:T(8,128)(2,1)S(1)} %copy-done.5), channel_id=1, source_target_pairs={{8,0},{16,8},{24,16},{32,24},{40,32},{48,40},{56,48},{64,56},{72,6... | collective-permute-start | bytes 49160 | tf_op jit(solution)/shard_map/ppermute | solution.py:427
  101.9 7.7 %collective-permute-start.3 = (bf16[64,128]{1,0:T(8,128)(2,1)S(1)}, bf16[64,128]{1,0:T(8,128)(2,1)S(1)}, u32[]{:S(2)}, u32[]{:S(2)}) collective-permute-start(bf16[64,128]{1,0:T(8,128)(2,1)S(1)} %copy-done.4), channel_id=1, source_target_pairs={{0,8},{8,16},{16,24},{24,32},{32,40},{40,48},{48,56},{56,64},{64,7... | collective-permute-start | bytes 49160 | tf_op jit(solution)/shard_map/ppermute | solution.py:428
  103.8 5.8 %copy-start.6 = (bf16[64,128]{1,0:T(8,128)(2,1)}, bf16[64,128]{1,0:T(8,128)(2,1)S(1)}, u32[]{:S(2)}) copy-start(bf16[64,128]{1,0:T(8,128)(2,1)S(1)} %collective-permute-done.2.from_above_ref) | copy-start | bytes 49156
  109.6 0.6 copy-start.7
  112.9 0.7 copy-start

commit v2 on v1

--- a/solution.py
+++ b/solution.py
@@ -13,11 +13,12 @@
 F32 = jnp.float32
 BF16 = jnp.bfloat16
 TILE = 256
-VMEM_LIMIT = 56 * 1024 * 1024
-
-ROWS_ONE = 48
-ROWS_TWO = 176
-GRAD_ROWS = 128
+MIB = 1024 * 1024
+
+PAIR = ("y0", "sub")
+PLANE = ("y1", "y0", "sub")
+HEAD = 32
+GRAD_ROWS = 1024
 
 
 def mm(a, b):
@@ -64,14 +65,21 @@
     return onehot(column == iota((column.shape[0], width), 1))
 
 
-def face_kernel(node_ref, bound_ref, pick_ref, down_ref, up_ref):
-    node = node_ref[...]
-    for k, out_ref in ((0, down_ref), (1, up_ref)):
-        column = face_column(bound_ref[k : k + 1, :], pick_ref[k])
-        out_ref[...] = mm(onehot_rows(column, node.shape[0]), node).astype(BF16)
-
-
-def send_kernel(node_ref, intra_ref, second_ref, coarse_cot_ref, below_ref, above_ref, out_ref):
+def slab_in_plane():
+    return lax.axis_index("y1") * lax.axis_size("y0") + lax.axis_index("y0")
+
+
+def picked_rows(node, bound_ref, pick_ref, side):
+    face_row = jnp.where(side == 0, bound_ref[0:1, :], bound_ref[1:2, :])
+    return mm(onehot_rows(face_column(face_row, pick_ref[side]), node.shape[0]), node)
+
+
+def face_kernel(node_ref, bound_ref, pick_ref, out_ref):
+    out_ref[...] = picked_rows(node_ref[...], bound_ref, pick_ref, lax.axis_index("y0")).astype(BF16)
+
+
+def send_kernel(node_ref, intra_ref, second_ref, coarse_cot_ref, bound_ref, pick_ref, out_ref):
+    odd = lax.axis_index("y0")
     node = node_ref[...]
     cells, feature = node.shape
     peers, halo = intra_ref.shape
@@ -80,14 +88,17 @@
     half = 0.5 * coarse_cot_ref[...].astype(F32)
     pool_rows = 16 * peers
     pool = mm(onehot(second_ref[...] - cells == iota((pool_rows, coarse), 0)), half.astype(BF16))
-    parts = [
+    same = [
         intra.reshape(peers, halo, feature),
-        below_ref[...].astype(F32).reshape(peers, halo, feature),
-        above_ref[...].astype(F32).reshape(peers, halo, feature),
         jnp.zeros((peers, halo, feature), F32),
         pool.reshape(peers, 16, feature),
     ]
-    out_ref[...] = jnp.concatenate(parts, axis=1).astype(BF16)
+    other = [
+        picked_rows(node, bound_ref, pick_ref, 1 - odd).reshape(peers, halo, feature),
+        jnp.zeros((peers, HEAD - halo, feature), F32),
+    ]
+    out_ref[pl.ds(peers * odd, peers)] = jnp.concatenate(same, axis=1).astype(BF16)
+    out_ref[pl.ds(peers * (1 - odd), peers)] = jnp.concatenate(other, axis=1).astype(BF16)
 
 
 def silu_parts(pre):
@@ -128,16 +139,21 @@
 ):
     cells, feature = node_ref.shape
     slots = edges_ref.shape[0]
-    peers = recv_ref.shape[0]
+    peers = recv_ref.shape[0] // 2
     tiles = slots // TILE
     count = count_ref[0, 0]
     node = node_ref[...]
-    received = recv_ref[...].astype(F32)
+    odd = lax.axis_index("y0")
+    same = recv_ref[pl.ds(peers * odd, peers)]
+    near = same.astype(F32)
+    other = recv_ref[pl.ds(peers * (1 - odd), peers)].astype(F32)[:, 0:8, :]
+    passed = near[:, 8:16, :]
+    kinds = [near[:, 0:8, :], jnp.where(odd == 0, passed, other), jnp.where(odd == 0, other, passed)]
     halo_rows = 3 * 8 * peers
     wide = table_ref.shape[0]
     table_ref[0:cells, :] = node
     halo = jnp.concatenate(
-        [received[:, 8 * k : 8 * k + 8, :].reshape(8 * peers, feature) for k in range(3)]
+        [rows.reshape(8 * peers, feature) for rows in kinds]
         + [jnp.zeros((wide - cells - halo_rows, feature), F32)],
         axis=0,
     )
@@ -207,7 +223,7 @@
     half = (0.5 * coarse_cot_ref[...].astype(F32)).astype(BF16)
     cell_row = iota((cells, coarse), 0)
     pooled = onehot((first_ref[...] == cell_row) | (second_ref[...] == cell_row))
-    returned = recv_ref[:, ROWS_ONE - 16 : ROWS_ONE, :].reshape(16 * peers, feature)
+    returned = same[:, 16:32, :].reshape(16 * peers, feature)
     hot_match = onehot_rows(column_of(match_ref[...]), cells)
     d_fresh = mm(pooled, half) + mm_tn(hot_match, returned)
     match_rows = mm(hot_match, fresh)
@@ -271,51 +287,55 @@
         d_table[cells + 8 * peers * k : cells + 8 * peers * (k + 1), :].reshape(peers, 8, feature)
         for k in range(3)
     ]
-    parts = kinds + [
-        jnp.zeros((peers, 8, feature), F32),
-        match_rows.reshape(peers, 16, feature),
-        grads_ref[...].reshape(peers, GRAD_ROWS, feature),
-    ]
-    send_ref[...] = jnp.concatenate(parts, axis=1).astype(BF16)
-
-
-def split_kernel(recv_ref, down_ref, up_ref, sum_ref):
-    peers, _, feature = recv_ref.shape
-    head = recv_ref[:, 0:32, :].astype(F32)
-    down_ref[...] = head[:, 8:16, :].reshape(8 * peers, feature).astype(BF16)
-    up_ref[...] = head[:, 16:24, :].reshape(8 * peers, feature).astype(BF16)
-    total = recv_ref[0, 48:, :].astype(F32)
-    for p in range(1, peers):
-        total = total + recv_ref[p, 48:, :].astype(F32)
-    total = total.astype(BF16)
-    for p in range(sum_ref.shape[0]):
-        sum_ref[p] = total
-
-
-def add_kernel(scale, recv_ref, out_ref):
-    total = recv_ref[0].astype(F32)
-    for p in range(1, recv_ref.shape[0]):
-        total = total + recv_ref[p].astype(F32)
-    total = (total * scale).astype(BF16)
-    for p in range(out_ref.shape[0]):
-        out_ref[p] = total
+    slab = slab_in_plane()
+    slabs = send_ref.shape[0] // peers
+    pad = [jnp.zeros((peers, HEAD - 8, feature), F32)]
+    blank = jnp.zeros((peers, HEAD, feature), BF16)
+    for y in range(slabs):
+        send_ref[peers * y : peers * (y + 1), 0:HEAD, :] = blank
+    onward = jnp.where(slab == 0, kinds[1], kinds[2])
+    same = [kinds[0], onward, match_rows.reshape(peers, 16, feature)]
+    send_ref[pl.ds(peers * slab, peers), 0:HEAD, :] = jnp.concatenate(same, axis=1).astype(BF16)
+
+    @pl.when(slab > 0)
+    def _():
+        rows = jnp.concatenate([kinds[1]] + pad, axis=1).astype(BF16)
+        send_ref[pl.ds(peers * (slab - 1), peers), 0:HEAD, :] = rows
+
+    @pl.when(slab < slabs - 1)
+    def _():
+        rows = jnp.concatenate([kinds[2]] + pad, axis=1).astype(BF16)
+        send_ref[pl.ds(peers * (slab + 1), peers), 0:HEAD, :] = rows
+
+    share = GRAD_ROWS // (slabs * peers)
+    grads = grads_ref[...].reshape(slabs * peers, share, feature)
+    send_ref[:, HEAD:, :] = grads.astype(BF16)
 
 
 def finish_kernel(
-    recv_ref, from_above_ref, from_below_ref, d_node_ref, fresh_ref, intra_ref, bound_ref,
+    recv_ref, passed_ref, d_node_ref, fresh_ref, intra_ref, bound_ref,
     pick_ref, first_ref, second_ref, d_out_ref, coarse_ref,
 ):
-    peers, _, feature = recv_ref.shape
-    cells = d_node_ref.shape[0]
-    head = recv_ref[:, 0:16, :].astype(F32)
-    own = head[:, 0:8, :].reshape(8 * peers, feature).astype(BF16)
+    peers = intra_ref.shape[0]
+    slabs = recv_ref.shape[0] // peers
+    cells, feature = d_node_ref.shape
+    slab = slab_in_plane()
+    same = recv_ref[pl.ds(peers * slab, peers), 0:HEAD, :]
+
+    def gradients(block):
+        return block.astype(F32)[:, 0:8, :].reshape(8 * peers, feature).astype(BF16)
+
     hot = onehot_rows(column_of(intra_ref[...]), cells)
-    total = mm_tn(hot, own)
-    for k, back_ref in ((0, from_below_ref), (1, from_above_ref)):
+    total = mm_tn(hot, gradients(same))
+    passed = passed_ref[...]
+    lower = jnp.maximum(slab - 1, 0)
+    upper = jnp.minimum(slab + 1, slabs - 1)
+    for k, near, edge in ((0, lower, slab == 0), (1, upper, slab == slabs - 1)):
         column = face_column(bound_ref[k : k + 1, :], pick_ref[k])
-        total = total + mm_tn(onehot_rows(column, cells), back_ref[...])
+        direct = gradients(recv_ref[pl.ds(peers * near, peers), 0:HEAD, :])
+        total = total + mm_tn(onehot_rows(column, cells), jnp.where(edge, passed, direct))
     d_out_ref[...] = d_node_ref[...] + total
-    partners = recv_ref[:, 32:48, :].reshape(16 * peers, feature)
+    partners = same[:, 16:32, :].reshape(16 * peers, feature)
     coarse = coarse_ref.shape[0]
     cell_row = iota((cells, coarse), 0)
     near = onehot((first_ref[...] == cell_row) | (second_ref[...] == cell_row))
@@ -324,20 +344,17 @@
 
 
 def unpack_kernel(recv_ref, w1_ref, w2_ref, nw1_ref, nw2_ref, b1_ref, g_ref, nb1_ref, ng_ref):
-    for p in range(3):
-        w1_ref[128 * p : 128 * p + 128, :] = recv_ref[p].astype(F32)
-    w2_ref[...] = recv_ref[3].astype(F32)
-    nw1_ref[0:128, :] = recv_ref[4].astype(F32)
-    nw1_ref[128:256, :] = recv_ref[5].astype(F32)
-    nw2_ref[...] = recv_ref[6].astype(F32)
-    tail = recv_ref[7, 0:16, :].astype(F32)
-    b1_ref[...] = tail[0:1, :]
-    g_ref[...] = tail[1:2, :]
-    nb1_ref[...] = tail[2:3, :]
-    ng_ref[...] = tail[3:4, :]
-
-
-def call(kernel, out_shape, *args, scratch=(), smem=(), name=None, cost=None):
+    start = 0
+    for out_ref in (w1_ref, w2_ref, nw1_ref, nw2_ref):
+        rows = out_ref.shape[0]
+        out_ref[...] = recv_ref[start : start + rows, :].astype(F32)
+        start += rows
+    tail = recv_ref[start : start + 16, :].astype(F32)
+    for k, out_ref in enumerate((b1_ref, g_ref, nb1_ref, ng_ref)):
+        out_ref[...] = tail[k : k + 1, :]
+
+
+def call(kernel, out_shape, *args, scratch=(), smem=(), name=None, cost=None, mib=8):
     specs = [
         pl.BlockSpec(memory_space=pltpu.SMEM if i in smem else pltpu.VMEM) for i in range(len(args))
     ]
@@ -347,7 +364,7 @@
         in_specs=specs,
         out_specs=jax.tree.map(lambda _: pl.BlockSpec(memory_space=pltpu.VMEM), out_shape),
         scratch_shapes=list(scratch),
-        compiler_params=pltpu.CompilerParams(vmem_limit_bytes=VMEM_LIMIT),
+        compiler_params=pltpu.CompilerParams(vmem_limit_bytes=mib * MIB),
         name=name,
         cost_estimate=cost,
     )(*args)
@@ -370,21 +387,29 @@
     slots = edges.shape[0]
     coarse = coarse_cot.shape[0]
     peers = lax.axis_size("sub")
-    planes, columns = lax.axis_size("z"), lax.axis_size("y")
-    dom = ("z", "y")
-    upward = [(i, i + 1) for i in range(slabs - 1)]
-    downward = [(i + 1, i) for i in range(slabs - 1)]
+    planes = lax.axis_size("z")
+    in_plane = slabs // planes
+    dom = ("z", "y1", "y0")
     face = shape_of((8 * peers, feature), BF16)
     wide = -(-(cells + 24 * peers) // 256) * 256
 
-    to_down, to_up = call(face_kernel, (face, face), node, bound, pick, name="faces")
-    from_below = lax.ppermute(to_up, dom, upward)
-    from_above = lax.ppermute(to_down, dom, downward)
+    def swap(rows, step):
+        pairs = [(i - 1, i) for i in range(step, slabs, step)]
+        return lax.ppermute(rows, dom, pairs + [(j, i) for i, j in pairs])
+
+    def exchange(blocks, axes):
+        return lax.all_to_all(blocks, axes, split_axis=0, concat_axis=0, tiled=True)
+
+    passed = swap(call(face_kernel, face, node, bound, pick, name="faces"), 2)
     sent = call(
-        send_kernel, shape_of((peers, ROWS_ONE, feature), BF16),
-        node, intra, second, coarse_cot, from_below, from_above, name="send",
-    )
-    received = lax.all_to_all(sent, "sub", split_axis=0, concat_axis=0, tiled=True)
+        send_kernel, shape_of((2 * peers, HEAD, feature), BF16),
+        node, intra, second, coarse_cot, bound, pick, name="send",
+        cost=pl.CostEstimate(flops=60_000_000, bytes_accessed=400_000, transcendentals=0),
+    )
+    sent = lax.dynamic_update_slice(
+        sent, passed.reshape(peers, 8, feature), (peers * lax.axis_index("y0"), 8, 0)
+    )
+    received = exchange(sent, PAIR)
 
     new_edges, d_edges, d_node, fresh, sent = call(
         main_kernel,
@@ -393,7 +418,7 @@
             shape_of((slots, feature), BF16),
             shape_of((cells, feature), F32),
             shape_of((cells, feature), BF16),
-            shape_of((peers, ROWS_TWO, feature), BF16),
+            shape_of((in_plane * peers, HEAD + GRAD_ROWS // (in_plane * peers), feature), BF16),
         ),
         edge_count, src, dst, node, received, edges, edge_cot, coarse_cot, first, second, match,
         edge_w1, edge_b1[None], edge_w2, edge_gain[None],
@@ -415,34 +440,29 @@
             pltpu.VMEM((feature, feature), F32),
             pltpu.VMEM((8, feature), F32),
             pltpu.VMEM((8, feature), F32),
-            pltpu.VMEM((peers * GRAD_ROWS, feature), F32),
+            pltpu.VMEM((GRAD_ROWS, feature), F32),
         ),
         name="layer",
-    )
-    received = lax.all_to_all(sent, "sub", split_axis=0, concat_axis=0, tiled=True)
-    piece = (GRAD_ROWS, feature)
-    back_down, back_up, partial = call(
-        split_kernel, (face, face, shape_of((planes,) + piece, BF16)), received, name="split"
-    )
-    from_above = lax.ppermute(back_down, dom, downward)
-    from_below = lax.ppermute(back_up, dom, upward)
-    partial = lax.all_to_all(partial, "z", split_axis=0, concat_axis=0, tiled=True)
+        mib=24,
+    )
+    received = exchange(sent, PLANE)
+    onward = lax.dynamic_slice(received, (peers * slab_in_plane(), 8, 0), (peers, 8, feature))
+    passed = swap(onward.reshape(8 * peers, feature), in_plane)
+    scale = 1.0 / math.sqrt(slabs * peers * slots)
+
+    def total(blocks, factor, copies):
+        rows = (jnp.sum(blocks.astype(F32), axis=0) * factor).astype(BF16)
+        return jnp.broadcast_to(rows, (copies,) + rows.shape)
+
+    summed = exchange(total(received[:, HEAD:], 1.0, planes), "z")
+    grads = exchange(total(summed, scale, in_plane * peers), PLANE)
     d_node, coarse_out = call(
         finish_kernel,
         (shape_of((cells, feature), F32), shape_of((coarse, feature), BF16)),
-        received, from_above, from_below, d_node, fresh, intra, bound, pick, first, second,
+        received, passed, d_node, fresh, intra, bound, pick, first, second,
         name="finish",
         cost=pl.CostEstimate(flops=300_000_000, bytes_accessed=2_000_000, transcendentals=0),
     )
-    partial = call(
-        functools.partial(add_kernel, 1.0), shape_of((columns,) + piece, BF16), partial, name="add_z"
-    )
-    partial = lax.all_to_all(partial, "y", split_axis=0, concat_axis=0, tiled=True)
-    scale = 1.0 / math.sqrt(slabs * peers * slots)
-    partial = call(
-        functools.partial(add_kernel, scale), shape_of((peers,) + piece, BF16), partial, name="add_y"
-    )
-    grads = lax.all_to_all(partial, "sub", split_axis=0, concat_axis=0, tiled=True)
     row = shape_of((1, feature), F32)
     w1, w2, nw1, nw2, b1, g, nb1, ng = call(
         unpack_kernel,
@@ -453,7 +473,7 @@
             shape_of((feature, feature), F32),
             row, row, row, row,
         ),
-        grads,
+        grads.reshape(GRAD_ROWS, feature),
         name="unpack",
     )
     return (
@@ -464,9 +484,9 @@
 
 def solution(mesh):
     slabs, peers = mesh.shape["dom"], mesh.shape["sub"]
-    columns = 4 if slabs % 8 == 0 else 2
-    inner = Mesh(mesh.devices.reshape(slabs // columns, columns, peers), ("z", "y", "sub"))
-    dom = ("z", "y")
+    devices = mesh.devices.reshape(slabs // 4, 2, 2, peers)
+    dom = ("z", "y1", "y0")
+    inner = Mesh(devices, dom + ("sub",))
     four, three = P(dom, "sub", None, None), P(dom, "sub", None)
     return jax.shard_map(
         functools.partial(per_device, slabs),

time: 116 us -> 99.8 us (0.86)
  the two profiles are of different devices: /device:TPU:34 before, /device:TPU:1 now
where the time goes in v2:
time: 99.8 us; the launch traced here: 98.8 us
  blocking collectives  33 us (33%)
  Pallas kernels  22.3 us (22%)
  starting transfers between devices  16.5 us (17%)
  local copies, waits for them, and re-layouts  13.9 us (14%)
  waiting for transfers between devices  11.5 us (12%)
  between operations  1.49 us (1%)
    all_to_all x2, blocking collectives, exchange(): return lax.all_to_all(blocks, axes, split_axis=0, concat_axis=0, tiled=True)  33 us
    pallas_call x5, Pallas kernels, call(): pl.pallas_call(kernel, out_shape=out_shape, in_specs=specs, out_specs=jax...  22.3 us
    all_to_all x2, starting transfers between devices, exchange(): return lax.all_to_all(blocks, axes, split_axis=0, concat_axis=0, tiled=True)  15.2 us
    unnamed x52, local copies, waits for them, and re-layouts  12.6 us
    all_to_all x2, waiting for transfers between devices, exchange(): return lax.all_to_all(blocks, axes, split_axis=0, concat_axis=0, tiled=True)  11.5 us
  transfers between devices with their start and end apart: 4, of which 2 were waited for; matrix products, arithmetic and copies ran while one was open for 0% of the time, Pallas kernels for 2%

profile of v2, /device:TPU:1, one launch (start us, length us, event | category | flops | bytes accessed | tf_op | source)
XLA Modules:
  0.0 98.8 jit_solution(12622544208516818729)
XLA Ops:
  0.7 0.9 copy-done
  1.6 0.7 copy-done.10
  2.3 0.7 copy-done.18
  3.0 0.3 faces.1
  3.3 0.7 collective-permute-start
  4.0 0.8 copy-done.4
  4.8 0.7 copy-done.11
  5.5 0.7 copy-done.19
  6.2 1.0 send.1
  7.2 0.6 bitcast_dynamic-update-slice_fusion
  7.8 9.8 %all-to-all-start = ((bf16[16,32,128]{2,1,0:T(8,128)(2,1)}), bf16[16,32,128]{2,1,0:T(8,128)(2,1)S(1)}, u32[]{:S(2)}, u32[]{:S(2)}) async-start(bf16[16,32,128]{2,1,0:T(8,128)(2,1)} %bitcast_dynamic-update-slice_fusion), calls=%async_computation | async-start | bytes 262144 | tf_op jit(solution)/shard_map/all_to_all | solution.py:401
  18.2 5.4 %all-to-all-done.recv_ref = bf16[16,32,128]{2,1,0:T(8,128)(2,1)S(1)} async-done(((bf16[16,32,128]{2,1,0:T(8,128)(2,1)}), bf16[16,32,128]{2,1,0:T(8,128)(2,1)S(1)}, u32[]{:S(2)}, u32[]{:S(2)}) %all-to-all-start) | async-done | bytes 131104 | tf_op jit(solution)/shard_map/all_to_all | solution.py:401
  23.7 0.7 copy-done.14
  24.4 1.0 %copy-done.3 = bf16[1,1,2048,128]{3,2,1,0:T(8,128)(2,1)S(1)} copy-done((bf16[1,1,2048,128]{3,2,1,0:T(8,128)(2,1)S(1)}, bf16[1,1,2048,128]{3,2,1,0:T(8,128)(2,1)}, u32[]{:S(2)}) %copy-start.3) | copy-done | bytes 524312
  25.4 0.8 copy-done.7
  26.3 0.8 copy-done.8
  27.0 0.8 copy-done.9
  27.8 0.7 copy-done.15
  28.5 0.7 copy-done.22
  29.1 0.7 copy-done.23
  29.8 0.7 copy-done.24
  30.4 0.7 copy-done.25
  31.1 18.7 %layer.1 = (bf16[2048,128]{1,0:T(8,128)(2,1)}, bf16[2048,128]{1,0:T(8,128)(2,1)}, f32[512,128]{1,0:T(8,128)S(1)}, bf16[512,128]{1,0:T(8,128)(2,1)S(1)}, bf16[32,64,128]{2,1,0:T(8,128)(2,1)S(1)}) custom-call(s32[1,1]{1,0:T(1,128)S(6)} %copy.34.count_ref, s32[1,2048]{1,0:T(1,128)S(1)} %bitcast.40, s32[1,2048]{1,0:T(1,128)S(1)} %bitcast.41, ...), custom_call_target="tpu_custom_call" | custom-call | tf_op jit(solution)/shard_map/layer/pallas_call | solution.py:361
  49.8 17.8 %all_to_all.20.recv_ref = bf16[32,64,128]{2,1,0:T(8,128)(2,1)S(1)} all-to-all(bf16[32,64,128]{2,1,0:T(8,128)(2,1)S(1)} %get-tuple-element.28), channel_id=1, replica_groups=mesh['z'=8,'y1'=2,'y0'=2,'sub'=8] {'y1','y0','sub'}, dimensions={0} | all-to-all | bytes 1048576 | tf_op jit(solution)/shard_map/all_to_all | solution.py:401
  67.7 15.2 %all_to_all.21 = bf16[8,32,128]{2,1,0:T(8,128)(2,1)S(1)} all-to-all(bf16[8,32,128]{2,1,0:T(8,128)(2,1)S(1)} %broadcast_in_dim.38), channel_id=1, replica_groups=mesh['z'=8,'y1'=2,'y0'=2,'sub'=8] {'z'}, dimensions={0} | all-to-all | bytes 131072 | tf_op jit(solution)/shard_map/all_to_all | solution.py:401
  82.9 0.7 broadcast_in_dim.39
  83.6 5.4 %all-to-all-start.3 = ((bf16[32,32,128]{2,1,0:T(8,128)(2,1)}), bf16[32,32,128]{2,1,0:T(8,128)(2,1)S(1)}, u32[]{:S(2)}, u32[]{:S(2)}) async-start(bf16[32,32,128]{2,1,0:T(8,128)(2,1)} %broadcast_in_dim.39), calls=%async_computation.3 | async-start | bytes 524288 | tf_op jit(solution)/shard_map/all_to_all | solution.py:401
  89.1 0.7 collective-permute-start.1
  89.8 0.7 copy-done.20
  90.4 1.5 %finish.1 = (f32[512,128]{1,0:T(8,128)}, bf16[256,128]{1,0:T(8,128)(2,1)}) custom-call(bf16[32,64,128]{2,1,0:T(8,128)(2,1)S(1)} %all_to_all.20.recv_ref, bf16[64,128]{1,0:T(8,128)(2,1)S(1)} %collective-permute-done.1.passed_ref, f32[512,128]{1,0:T(8,128)S(1)} %get-tuple-element.29.d_node_ref, bf16[512,128]{1,0:T(8,128)(2,1)S(1)} %get-tuple-element.30.fresh_ref, ...), custom_call_target="tpu_custom_call" | custom-call | flops 300000000 | bytes 2000000 | tf_op jit(solution)/shard_map/finish/pallas_call | solution.py:361
  92.0 6.1 %all-to-all-done.3 = bf16[32,32,128]{2,1,0:T(8,128)(2,1)S(1)} async-done(((bf16[32,32,128]{2,1,0:T(8,128)(2,1)}), bf16[32,32,128]{2,1,0:T(8,128)(2,1)S(1)}, u32[]{:S(2)}, u32[]{:S(2)}) %all-to-all-start.3) | async-done | bytes 262176 | tf_op jit(solution)/shard_map/all_to_all | solution.py:401
  98.0 0.8 unpack.1
  (42 shorter events, 0.2 us)
Async XLA Ops:
  0.6 3.3 %copy-start.16 = (s32[1,1,8,8]{3,2,1,0:T(8,128)S(1)}, s32[1,1,8,8]{3,2,1,0:T(8,128)}, u32[]{:S(2)}) copy-start(s32[1,1,8,8]{3,2,1,0:T(8,128)} %param.26) | copy-start | bytes 772
  0.7 3.3 %copy-start.17 = (s32[1,1,256]{2,1,0:T(1,128)S(1)}, s32[1,1,256]{2,1,0:T(1,128)}, u32[]{:S(2)}) copy-start(s32[1,1,256]{2,1,0:T(1,128)} %param.31) | copy-start | bytes 3076
  0.7 0.9 copy-start
  1.6 0.7 copy-start.10
  2.3 0.7 copy-start.18
  3.0 1.0 %copy-start.1 = (bf16[1,1,512,128]{3,2,1,0:T(8,128)(2,1)S(1)}, bf16[1,1,512,128]{3,2,1,0:T(8,128)(2,1)}, u32[]{:S(2)}) copy-start(bf16[1,1,512,128]{3,2,1,0:T(8,128)(2,1)} %param.21) | copy-start | bytes 393220
  3.0 20.7 %copy-start.2 = (bf16[1,1,2048,128]{3,2,1,0:T(8,128)(2,1)S(1)}, bf16[1,1,2048,128]{3,2,1,0:T(8,128)(2,1)}, u32[]{:S(2)}) copy-start(bf16[1,1,2048,128]{3,2,1,0:T(8,128)(2,1)} %param.22) | copy-start | bytes 1572868
  3.3 3.9 %collective-permute-start = (bf16[64,128]{1,0:T(8,128)(2,1)S(1)}, bf16[64,128]{1,0:T(8,128)(2,1)S(1)}, u32[]{:S(2)}, u32[]{:S(2)}) collective-permute-start(bf16[64,128]{1,0:T(8,128)(2,1)S(1)} %faces.1), channel_id=1, source_target_pairs={{8,16},{24,32},{40,48},{56,64},{72,80},{88,96},{104,112},{120,128}... | collective-permute-start | bytes 49160 | tf_op jit(solution)/shard_map/ppermute | solution.py:398
  4.0 0.8 copy-start.4
  4.8 0.7 copy-start.11
  5.5 0.7 copy-start.19
  7.8 15.9 %copy-start.5 = (bf16[1,1,256,128]{3,2,1,0:T(8,128)(2,1)S(1)}, bf16[1,1,256,128]{3,2,1,0:T(8,128)(2,1)}, u32[]{:S(2)}) copy-start(bf16[1,1,256,128]{3,2,1,0:T(8,128)(2,1)} %param.41) | copy-start | bytes 196612
  7.8 15.9 %copy-start.6 = (bf16[384,128]{1,0:T(8,128)(2,1)S(1)}, bf16[384,128]{1,0:T(8,128)(2,1)}, u32[]{:S(2)}) copy-start(bf16[384,128]{1,0:T(8,128)(2,1)} %ew1_ref.1) | copy-start | bytes 294916
  7.8 15.9 %all-to-all-start = ((bf16[16,32,128]{2,1,0:T(8,128)(2,1)}), bf16[16,32,128]{2,1,0:T(8,128)(2,1)S(1)}, u32[]{:S(2)}, u32[]{:S(2)}) async-start(bf16[16,32,128]{2,1,0:T(8,128)(2,1)} %bitcast_dynamic-update-slice_fusion), calls=%async_computation | async-start | bytes 262144 | tf_op jit(solution)/shard_map/all_to_all | solution.py:401
  23.7 0.7 copy-start.14
  23.7 0.7 copy-start.13
  23.7 0.7 copy-start.21
  24.4 1.0 %copy-start.3 = (bf16[1,1,2048,128]{3,2,1,0:T(8,128)(2,1)S(1)}, bf16[1,1,2048,128]{3,2,1,0:T(8,128)(2,1)}, u32[]{:S(2)}) copy-start(bf16[1,1,2048,128]{3,2,1,0:T(8,128)(2,1)} %param.40) | copy-start | bytes 1572868
  25.4 0.8 copy-start.7
  26.3 0.8 copy-start.8
  27.0 0.8 copy-start.9
  27.8 0.7 copy-start.15
  28.5 0.7 copy-start.22
  29.1 0.7 copy-start.23
  29.8 0.7 copy-start.24
  30.4 0.7 copy-start.25
  83.6 14.4 %all-to-all-start.3 = ((bf16[32,32,128]{2,1,0:T(8,128)(2,1)}), bf16[32,32,128]{2,1,0:T(8,128)(2,1)S(1)}, u32[]{:S(2)}, u32[]{:S(2)}) async-start(bf16[32,32,128]{2,1,0:T(8,128)(2,1)} %broadcast_in_dim.39), calls=%async_computation.3 | async-start | bytes 524288 | tf_op jit(solution)/shard_map/all_to_all | solution.py:401
  89.0 0.7 copy-start.12
  89.1 0.7 collective-permute-start.1
  89.7 0.7 copy-start.20

commit v3 on v2

--- a/solution.py
+++ b/solution.py
@@ -12,7 +12,8 @@
 NORM_EPSILON = 1e-05
 F32 = jnp.float32
 BF16 = jnp.bfloat16
-TILE = 256
+TILE = 2048
+UNROLL = 1
 MIB = 1024 * 1024
 
 PAIR = ("y0", "sub")
@@ -108,35 +109,75 @@
     return act, slope
 
 
-def norm_forward(out):
-    centred = out - jnp.mean(out, axis=1, keepdims=True)
-    inv = lax.rsqrt(jnp.mean(centred * centred, axis=1, keepdims=True) + NORM_EPSILON)
+def norm_forward(out, axis):
+    centred = out - jnp.mean(out, axis=axis, keepdims=True)
+    inv = lax.rsqrt(jnp.mean(centred * centred, axis=axis, keepdims=True) + NORM_EPSILON)
     return centred * inv, inv
 
 
-def norm_backward(u, normed, inv, gain):
+def norm_backward(u, normed, inv, gain, axis):
     scaled = u * gain
     inner = (
         scaled
-        - jnp.mean(scaled, axis=1, keepdims=True)
-        - normed * jnp.mean(scaled * normed, axis=1, keepdims=True)
+        - jnp.mean(scaled, axis=axis, keepdims=True)
+        - normed * jnp.mean(scaled * normed, axis=axis, keepdims=True)
     )
     return inner * inv
 
 
-def fold_rows(x):
-    rows, feature = x.shape
-    return jnp.sum(x.reshape(rows // 8, 8, feature), axis=0)
+def fold_lanes(x):
+    total = x[:, 0:128]
+    for k in range(1, x.shape[1] // 128):
+        total = total + x[:, 128 * k : 128 * k + 128]
+    return total
+
+
+def column_block(row, width):
+    block = jnp.broadcast_to(row, (128, 128)).T
+    return jnp.concatenate([block] * (width // 128), axis=1)
+
+
+def hot_columns(ids, rows):
+    width = ids.shape[1]
+
+    def spread(x):
+        return jnp.broadcast_to(x.astype(F32), (16, width)).astype(BF16)
+
+    tens, units = spread(ids & -16), spread(ids & 15)
+    zero = jnp.zeros((16, width), BF16)
+    base = jnp.where(units == iota((16, width), 0).astype(F32).astype(BF16), jnp.ones((16, width), BF16), zero)
+    return jnp.concatenate(
+        [jnp.where(tens == jnp.full((16, width), 16 * r, BF16), base, zero) for r in range(rows // 16)], axis=0
+    )
 
 
 def main_kernel(
-    count_ref, src_ref, dst_ref, node_ref, recv_ref, edges_ref, cot_ref, coarse_cot_ref,
-    first_ref, second_ref, match_ref, ew1_ref, eb1_ref, ew2_ref, eg_ref,
-    nw1_ref, nb1_ref, nw2_ref, ng_ref,
-    new_edges_ref, d_edges_ref, d_node_ref, fresh_ref, send_ref,
-    table_ref, t2_ref, ohd_ref, oht_ref, agg_ref, act_ref, slope_ref, normed_ref, inv_ref,
-    dagg_ref, s_ref, dw1_ref, dw2_ref, db1_ref, dg_ref, grads_ref,
+    count_ref, recv_ref,
+    src_in, dst_in, node_in, ew1_in, edges_in, eb1_in, ew2_in, eg_in,
+    coarse_in, first_in, second_in, match_in, nw1_in, nb1_in, nw2_in, ng_in, cot_in,
+    new_edges_out, d_edges_out, d_node_ref, fresh_ref, send_ref,
+    src_ref, dst_ref, node_ref, ew1_ref, edges_ref, eb1_ref, ew2_ref, eg_ref,
+    coarse_cot_ref, first_ref, second_ref, match_ref, nw1_ref, nb1_ref, nw2_ref, ng_ref, cot_ref,
+    new_edges_ref, d_edges_ref,
+    table_ref, t2_ref, oht_ref, agg_ref, act_ref, slope_ref, normed_ref, inv_ref,
+    dagg_ref, s_ref, dw1_ref, dw2_ref, db1_ref, dg_ref, grads_ref, in_sem, out_sem,
 ):
+    sources = (
+        src_in, dst_in, node_in, ew1_in, edges_in, eb1_in, ew2_in, eg_in,
+        coarse_in, first_in, second_in, match_in, nw1_in, nb1_in, nw2_in, ng_in, cot_in,
+    )
+    targets = (
+        src_ref, dst_ref, node_ref, ew1_ref, edges_ref, eb1_ref, ew2_ref, eg_ref,
+        coarse_cot_ref, first_ref, second_ref, match_ref, nw1_ref, nb1_ref, nw2_ref, ng_ref, cot_ref,
+    )
+    copies = [
+        pltpu.make_async_copy(source, target, in_sem.at[k])
+        for k, (source, target) in enumerate(zip(sources, targets))
+    ]
+    for copy in copies:
+        copy.start()
+    for copy in copies[:8]:
+        copy.wait()
     cells, feature = node_ref.shape
     slots = edges_ref.shape[0]
     peers = recv_ref.shape[0] // 2
@@ -158,55 +199,49 @@
         axis=0,
     )
     table_ref[cells:wide, :] = halo.astype(BF16)
-    ew1_edge = ew1_ref[0:feature, :]
+    ew1_edge_t = ew1_ref[0:feature, :].T
     ew1_src = ew1_ref[feature : 2 * feature, :]
     ew1_dst = ew1_ref[2 * feature : 3 * feature, :]
-    high, low = two_parts(mm(table_ref[...], ew1_src))
-    t2_ref[0:wide, 0:feature] = high
-    t2_ref[0:wide, feature:] = low
-    high, low = two_parts(mm(node, ew1_dst) + eb1_ref[...])
-    t2_ref[wide:, 0:feature] = high
-    t2_ref[wide:, feature:] = low
+    high, low = two_parts(mm_nt(ew1_src.T, table_ref[...]))
+    t2_ref[0:feature, 0:wide] = high
+    t2_ref[feature:, 0:wide] = low
+    high, low = two_parts(mm_nt(ew1_dst.T, node) + column_block(eb1_ref[...], cells))
+    t2_ref[0:feature, wide:] = high
+    t2_ref[feature:, wide:] = low
     agg_ref[...] = jnp.zeros_like(agg_ref)
     ew2 = ew2_ref[...]
-    eg = eg_ref[...]
-
-    def live_of(start):
-        return iota((TILE, feature), 0) + start < count
+    ew2_t = ew2.T
+    eg = column_block(eg_ref[...], TILE)
 
     def forward_tile(i, carry):
         start = pl.multiple_of(i * TILE, TILE)
         rows = pl.ds(start, TILE)
-        src = src_ref[:, rows]
-        dst = dst_ref[:, rows]
-        src_col = jnp.broadcast_to(src, (128, TILE)).T
-        dst_col = jnp.broadcast_to(dst, (128, TILE)).T
-        lane = iota((TILE, 128), 1)
-        hot_src = jnp.concatenate(
-            [onehot(src_col == lane + 128 * k) for k in range(wide // 128)], axis=1
+        hot_src = hot_columns(src_ref[:, rows], wide)
+        hot_dst = hot_columns(dst_ref[:, rows], cells)
+        oht_ref[0:wide, rows] = hot_src
+        oht_ref[wide:, rows] = hot_dst
+        both = mm(t2_ref[:, 0:wide], hot_src) + mm(t2_ref[:, wide:], hot_dst)
+        edges = edges_ref[rows, :]
+        pre = both[0:feature] + both[feature:] + mm_nt(ew1_edge_t, edges)
+        act, slope = silu_parts(pre)
+        act_ref[:, rows] = act
+        slope_ref[:, rows] = slope
+        normed, inv = norm_forward(mm(ew2_t, act), 0)
+        normed_ref[:, rows] = normed
+        inv_ref[:, rows] = inv
+        message = jnp.where(iota((feature, TILE), 1) + start < count, normed * eg, 0.0)
+        fresh_edges = jnp.where(
+            iota((TILE, feature), 0) + start < count, edges.astype(F32) + message.T, 0.0
         )
-        hot_dst = jnp.concatenate(
-            [onehot(dst_col == lane + 128 * k) for k in range(cells // 128)], axis=1
-        )
-        ohd_ref[rows, :] = hot_dst
-        both = mm(hot_src, t2_ref[0:wide, :]) + mm(hot_dst, t2_ref[wide:, :])
-        edges = edges_ref[rows, :]
-        pre = both[:, 0:feature] + both[:, feature:] + mm(edges, ew1_edge)
-        act, slope = silu_parts(pre)
-        act_ref[rows, :] = act
-        slope_ref[rows, :] = slope
-        normed, inv = norm_forward(mm(act, ew2))
-        normed_ref[rows, :] = normed
-        inv_ref[rows, :] = inv
-        live = live_of(start)
-        message = jnp.where(live, normed * eg, 0.0)
-        new_edges_ref[rows, :] = jnp.where(live, edges.astype(F32) + message, 0.0).astype(BF16)
-        hot = onehot(dst == iota((cells, TILE), 0))
-        oht_ref[:, rows] = hot
-        agg_ref[...] += mm(hot, jnp.concatenate(two_parts(message), axis=1))
+        new_edges_ref[rows, :] = fresh_edges.astype(BF16)
+        agg_ref[...] += mm_nt(hot_dst, jnp.concatenate(two_parts(message), axis=0))
         return carry
 
-    lax.fori_loop(0, tiles, forward_tile, 0)
+    lax.fori_loop(0, tiles, forward_tile, 0, unroll=UNROLL)
+    edges_copy = pltpu.make_async_copy(new_edges_ref, new_edges_out, out_sem.at[0])
+    edges_copy.start()
+    for copy in copies[8:]:
+        copy.wait()
 
     aggregate = (agg_ref[:, 0:feature] + agg_ref[:, feature:]).astype(BF16)
     nw1_node = nw1_ref[0:feature, :]
@@ -215,7 +250,7 @@
     act, slope = silu_parts(pre)
     nw2 = nw2_ref[...]
     ng = ng_ref[...]
-    normed, inv = norm_forward(mm(act, nw2))
+    normed, inv = norm_forward(mm(act, nw2), 1)
     fresh = (node.astype(F32) + normed * ng).astype(BF16)
     fresh_ref[...] = fresh
 
@@ -228,7 +263,7 @@
     d_fresh = mm(pooled, half) + mm_tn(hot_match, returned)
     match_rows = mm(hot_match, fresh)
 
-    d_out = norm_backward(d_fresh, normed, inv, ng)
+    d_out = norm_backward(d_fresh, normed, inv, ng, 1)
     grads_ref[899:900, :] = jnp.sum(d_fresh * normed, axis=0, keepdims=True)
     d_out_half = d_out.astype(BF16)
     grads_ref[768:896, :] = mm_tn(act, d_out_half)
@@ -238,9 +273,9 @@
     grads_ref[512:640, :] = mm_tn(node, d_pre_half)
     grads_ref[640:768, :] = mm_tn(aggregate, d_pre_half)
     d_node_ref[...] = d_fresh + mm_nt(d_pre_half, nw1_node)
-    high, low = two_parts(mm_nt(d_pre_half, nw1_agg))
-    dagg_ref[:, 0:feature] = high
-    dagg_ref[:, feature:] = low
+    high, low = two_parts(mm_nt(nw1_agg, d_pre_half))
+    dagg_ref[0:feature, :] = high
+    dagg_ref[feature:, :] = low
 
     s_ref[...] = jnp.zeros_like(s_ref)
     dw1_ref[...] = jnp.zeros_like(dw1_ref)
@@ -251,30 +286,33 @@
     def backward_tile(i, carry):
         start = pl.multiple_of(i * TILE, TILE)
         rows = pl.ds(start, TILE)
-        both = mm(ohd_ref[rows, :], dagg_ref[...])
-        live = live_of(start)
-        cot = jnp.where(live, cot_ref[rows, :].astype(F32), 0.0)
-        u = jnp.where(live, cot + (both[:, 0:feature] + both[:, feature:]), 0.0)
-        normed = normed_ref[rows, :]
-        d_out_half = norm_backward(u, normed, inv_ref[rows, :], eg).astype(BF16)
-        dg_ref[...] += fold_rows(u * normed)
-        dw2_ref[...] += mm_tn(act_ref[rows, :], d_out_half)
-        d_pre = mm_nt(d_out_half, ew2) * slope_ref[rows, :]
-        db1_ref[...] += fold_rows(d_pre)
+        both = mm(dagg_ref[...], oht_ref[wide:, rows])
+        cot = jnp.where(
+            iota((TILE, feature), 0) + start < count, cot_ref[rows, :].astype(F32), 0.0
+        )
+        u = jnp.where(
+            iota((feature, TILE), 1) + start < count, cot.T + (both[0:feature] + both[feature:]), 0.0
+        )
+        normed = normed_ref[:, rows]
+        d_out_half = norm_backward(u, normed, inv_ref[:, rows], eg, 0).astype(BF16)
+        dg_ref[...] += fold_lanes(u * normed)
+        dw2_ref[...] += mm_nt(act_ref[:, rows], d_out_half)
+        d_pre = mm(ew2, d_out_half) * slope_ref[:, rows]
+        db1_ref[...] += fold_lanes(d_pre)
         d_pre_half = d_pre.astype(BF16)
-        d_edges_ref[rows, :] = (cot + mm_nt(d_pre_half, ew1_edge)).astype(BF16)
-        dw1_ref[...] += mm_tn(edges_ref[rows, :], d_pre_half)
-        hot = onehot(src_ref[:, rows] == iota((wide, TILE), 0))
-        s_ref[0:wide, :] += mm(hot, d_pre_half)
-        s_ref[wide:, :] += mm(oht_ref[:, rows], d_pre_half)
+        d_edges_ref[rows, :] = (cot + mm_tn(d_pre_half, ew1_edge_t)).astype(BF16)
+        dw1_ref[...] += mm(d_pre_half, edges_ref[rows, :])
+        s_ref[...] += mm_nt(oht_ref[:, rows], d_pre_half)
         return carry
 
-    lax.fori_loop(0, tiles, backward_tile, 0)
-
-    grads_ref[0:128, :] = dw1_ref[...]
+    lax.fori_loop(0, tiles, backward_tile, 0, unroll=UNROLL)
+    d_edges_copy = pltpu.make_async_copy(d_edges_ref, d_edges_out, out_sem.at[1])
+    d_edges_copy.start()
+
+    grads_ref[0:128, :] = dw1_ref[...].T
     grads_ref[384:512, :] = dw2_ref[...]
-    grads_ref[896:897, :] = jnp.sum(db1_ref[...], axis=0, keepdims=True)
-    grads_ref[897:898, :] = jnp.sum(dg_ref[...], axis=0, keepdims=True)
+    grads_ref[896:897, :] = jnp.sum(db1_ref[...].T, axis=0, keepdims=True)
+    grads_ref[897:898, :] = jnp.sum(dg_ref[...].T, axis=0, keepdims=True)
     grads_ref[900:, :] = jnp.zeros_like(grads_ref[900:, :])
     high, low = two_parts(s_ref[0:wide, :])
     table = table_ref[...]
@@ -310,6 +348,8 @@
     share = GRAD_ROWS // (slabs * peers)
     grads = grads_ref[...].reshape(slabs * peers, share, feature)
     send_ref[:, HEAD:, :] = grads.astype(BF16)
+    edges_copy.wait()
+    d_edges_copy.wait()
 
 
 def finish_kernel(
@@ -354,15 +394,19 @@
         out_ref[...] = tail[k : k + 1, :]
 
 
-def call(kernel, out_shape, *args, scratch=(), smem=(), name=None, cost=None, mib=8):
-    specs = [
-        pl.BlockSpec(memory_space=pltpu.SMEM if i in smem else pltpu.VMEM) for i in range(len(args))
-    ]
+def call(kernel, out_shape, *args, scratch=(), smem=(), hbm=(), hbm_out=(), name=None, cost=None, mib=8):
+    def space(i, far):
+        return pltpu.HBM if i in far else pltpu.VMEM
+
+    one = not isinstance(out_shape, tuple)
+    outs = [pl.BlockSpec(memory_space=space(i, hbm_out)) for i in range(1 if one else len(out_shape))]
     return pl.pallas_call(
         kernel,
         out_shape=out_shape,
-        in_specs=specs,
-        out_specs=jax.tree.map(lambda _: pl.BlockSpec(memory_space=pltpu.VMEM), out_shape),
+        in_specs=[
+            pl.BlockSpec(memory_space=pltpu.SMEM if i in smem else space(i, hbm)) for i in range(len(args))
+        ],
+        out_specs=outs[0] if one else tuple(outs),
         scratch_shapes=list(scratch),
         compiler_params=pltpu.CompilerParams(vmem_limit_bytes=mib * MIB),
         name=name,
@@ -400,10 +444,10 @@
     def exchange(blocks, axes):
         return lax.all_to_all(blocks, axes, split_axis=0, concat_axis=0, tiled=True)
 
-    passed = swap(call(face_kernel, face, node, bound, pick, name="faces"), 2)
+    passed = swap(call(face_kernel, face, node, bound, pick, name="faces", mib=58), 2)
     sent = call(
         send_kernel, shape_of((2 * peers, HEAD, feature), BF16),
-        node, intra, second, coarse_cot, bound, pick, name="send",
+        node, intra, second, coarse_cot, bound, pick, name="send", mib=58,
         cost=pl.CostEstimate(flops=60_000_000, bytes_accessed=400_000, transcendentals=0),
     )
     sent = lax.dynamic_update_slice(
@@ -411,6 +455,10 @@
     )
     received = exchange(sent, PAIR)
 
+    far = (
+        src, dst, node, edge_w1, edges, edge_b1[None], edge_w2, edge_gain[None],
+        coarse_cot, first, second, match, node_w1, node_b1[None], node_w2, node_gain[None], edge_cot,
+    )
     new_edges, d_edges, d_node, fresh, sent = call(
         main_kernel,
         (
@@ -420,30 +468,34 @@
             shape_of((cells, feature), BF16),
             shape_of((in_plane * peers, HEAD + GRAD_ROWS // (in_plane * peers), feature), BF16),
         ),
-        edge_count, src, dst, node, received, edges, edge_cot, coarse_cot, first, second, match,
-        edge_w1, edge_b1[None], edge_w2, edge_gain[None],
-        node_w1, node_b1[None], node_w2, node_gain[None],
+        edge_count, received, *far,
         smem=(0,),
-        scratch=(
+        hbm=range(2, 2 + len(far)),
+        hbm_out=(0, 1),
+        scratch=[pltpu.VMEM(x.shape, x.dtype) for x in far]
+        + [
+            pltpu.VMEM((slots, feature), BF16),
+            pltpu.VMEM((slots, feature), BF16),
             pltpu.VMEM((wide, feature), BF16),
-            pltpu.VMEM((wide + cells, 2 * feature), BF16),
-            pltpu.VMEM((slots, cells), BF16),
-            pltpu.VMEM((cells, slots), BF16),
+            pltpu.VMEM((2 * feature, wide + cells), BF16),
+            pltpu.VMEM((wide + cells, slots), BF16),
             pltpu.VMEM((cells, 2 * feature), F32),
-            pltpu.VMEM((slots, feature), BF16),
-            pltpu.VMEM((slots, feature), F32),
-            pltpu.VMEM((slots, feature), F32),
-            pltpu.VMEM((slots, 1), F32),
-            pltpu.VMEM((cells, 2 * feature), BF16),
+            pltpu.VMEM((feature, slots), BF16),
+            pltpu.VMEM((feature, slots), F32),
+            pltpu.VMEM((feature, slots), F32),
+            pltpu.VMEM((1, slots), F32),
+            pltpu.VMEM((2 * feature, cells), BF16),
             pltpu.VMEM((wide + cells, feature), F32),
             pltpu.VMEM((feature, feature), F32),
             pltpu.VMEM((feature, feature), F32),
-            pltpu.VMEM((8, feature), F32),
-            pltpu.VMEM((8, feature), F32),
+            pltpu.VMEM((feature, feature), F32),
+            pltpu.VMEM((feature, feature), F32),
             pltpu.VMEM((GRAD_ROWS, feature), F32),
-        ),
+            pltpu.SemaphoreType.DMA((len(far),)),
+            pltpu.SemaphoreType.DMA((2,)),
+        ],
         name="layer",
-        mib=24,
+        mib=58,
     )
     received = exchange(sent, PLANE)
     onward = lax.dynamic_slice(received, (peers * slab_in_plane(), 8, 0), (peers, 8, feature))

time: 99.8 us -> 84.9 us (0.85)
  local copies, waits for them, and re-layouts: 13.9 us -> 2.68 us
  Pallas kernels: 22.3 us -> 17.4 us
  blocking collectives: 33 us -> 34.3 us
    unnamed x52 -> x16, local copies, waits for them, and re-layouts: 12.6 us -> 1.3 us
    pallas_call x5, Pallas kernels: 22.3 us -> 17.4 us  [call(): pl.pallas_call(kernel, out_shape=out_shape, in_specs=[pl.BlockSpec(memory...]
    all_to_all x2, blocking collectives: 33 us -> 34.3 us  [exchange(): return lax.all_to_all(blocks, axes, split_axis=0, concat_axis=0, tiled=True)]
where the time goes in v3:
time: 84.9 us; the launch traced here: 84.3 us
  blocking collectives  34.3 us (40%)
  Pallas kernels  17.4 us (20%)
  starting transfers between devices  16.9 us (20%)
  waiting for transfers between devices  11.5 us (14%)
  local copies, waits for them, and re-layouts  2.68 us (3%)
  between operations  1.46 us (2%)
    all_to_all x2, blocking collectives, exchange(): return lax.all_to_all(blocks, axes, split_axis=0, concat_axis=0, tiled=True)  34.3 us
    pallas_call x5, Pallas kernels, call(): pl.pallas_call(kernel, out_shape=out_shape, in_specs=[pl.BlockSpec(memory...  17.4 us
    all_to_all x2, starting transfers between devices, exchange(): return lax.all_to_all(blocks, axes, split_axis=0, concat_axis=0, tiled=True)  15.6 us
    all_to_all x2, waiting for transfers between devices, exchange(): return lax.all_to_all(blocks, axes, split_axis=0, concat_axis=0, tiled=True)  11.5 us
  transfers between devices with their start and end apart: 4, of which 2 were waited for; matrix products, arithmetic and copies ran while one was open for 0% of the time, Pallas kernels for 2%

profile of v3, /device:TPU:1, one launch (start us, length us, event | category | flops | bytes accessed | tf_op | source)
XLA Modules:
  0.0 84.3 jit_solution(13621042441567257279)
XLA Ops:
  0.6 1.8 %faces.1 = bf16[64,128]{1,0:T(8,128)(2,1)} custom-call(bf16[512,128]{1,0:T(8,128)(2,1)} %bitcast.43, s32[2,16]{1,0:T(2,128)} %bitcast.38, s32[2,8,8]{2,1,0:T(8,128)} %bitcast.30), custom_call_target="tpu_custom_call" | custom-call | tf_op jit(solution)/shard_map/faces/pallas_call | solution.py:403
  2.5 0.7 collective-permute-start
  3.2 1.9 %send.1 = bf16[16,32,128]{2,1,0:T(8,128)(2,1)} custom-call(bf16[512,128]{1,0:T(8,128)(2,1)} %bitcast.44, s32[8,8]{1,0:T(8,128)} %bitcast.33, s32[1,256]{1,0:T(1,128)} %bitcast.35, bf16[256,128]{1,0:T(8,128)(2,1)} %bitcast.48, s32[2,16]{1,0:T(2,128)} %bitcast.39, s32[2,8,8]{2,1,0:T(8,128)} %bitcast.31), custom_call_target="tpu_custom_call" | custom-call | flops 60000000 | bytes 400000 | tf_op jit(solution)/shard_map/send/pallas_call | solution.py:403
  5.1 0.0 collective-permute-done
  5.1 0.6 bitcast_dynamic-update-slice_fusion
  5.7 10.0 %all-to-all-start = ((bf16[16,32,128]{2,1,0:T(8,128)(2,1)}), bf16[16,32,128]{2,1,0:T(8,128)(2,1)S(1)}, u32[]{:S(2)}, u32[]{:S(2)}) async-start(bf16[16,32,128]{2,1,0:T(8,128)(2,1)} %bitcast_dynamic-update-slice_fusion), calls=%async_computation | async-start | bytes 262144 | tf_op jit(solution)/shard_map/all_to_all | solution.py:445
  16.4 5.4 %all-to-all-done.recv_ref = bf16[16,32,128]{2,1,0:T(8,128)(2,1)S(1)} async-done(((bf16[16,32,128]{2,1,0:T(8,128)(2,1)}), bf16[16,32,128]{2,1,0:T(8,128)(2,1)S(1)}, u32[]{:S(2)}, u32[]{:S(2)}) %all-to-all-start) | async-done | bytes 131104 | tf_op jit(solution)/shard_map/all_to_all | solution.py:445
  21.8 0.0 copy-start.7
  21.8 0.7 copy-done.7
  22.5 11.3 %layer.1 = (bf16[2048,128]{1,0:T(8,128)(2,1)}, bf16[2048,128]{1,0:T(8,128)(2,1)}, f32[512,128]{1,0:T(8,128)}, bf16[512,128]{1,0:T(8,128)(2,1)}, bf16[32,64,128]{2,1,0:T(8,128)(2,1)}) custom-call(s32[1,1]{1,0:T(1,128)S(6)} %copy.34.count_ref, bf16[16,32,128]{2,1,0:T(8,128)(2,1)} %copy-done.7, s32[1,2048]{1,0:T(1,128)} %bitcast.50, s32[1,2048]{1,0:T(1,128)} %bitcast.51, ...), custom_call_target="tpu_custom_call" | custom-call | tf_op jit(solution)/shard_map/layer/pallas_call | solution.py:403
  33.8 19.1 %all_to_all.20.recv_ref = bf16[32,64,128]{2,1,0:T(8,128)(2,1)S(1)} all-to-all(bf16[32,64,128]{2,1,0:T(8,128)(2,1)} %get-tuple-element.28), channel_id=1, replica_groups=mesh['z'=8,'y1'=2,'y0'=2,'sub'=8] {'y1','y0','sub'}, dimensions={0} | all-to-all | bytes 1048576 | tf_op jit(solution)/shard_map/all_to_all | solution.py:445
  53.0 15.2 %all_to_all.21 = bf16[8,32,128]{2,1,0:T(8,128)(2,1)S(1)} all-to-all(bf16[8,32,128]{2,1,0:T(8,128)(2,1)S(1)} %broadcast_in_dim.38), channel_id=1, replica_groups=mesh['z'=8,'y1'=2,'y0'=2,'sub'=8] {'z'}, dimensions={0} | all-to-all | bytes 131072 | tf_op jit(solution)/shard_map/all_to_all | solution.py:445
  68.2 0.7 broadcast_in_dim.39
  69.0 0.0 copy-start.5
  69.0 5.5 %all-to-all-start.3 = ((bf16[32,32,128]{2,1,0:T(8,128)(2,1)}), bf16[32,32,128]{2,1,0:T(8,128)(2,1)S(1)}, u32[]{:S(2)}, u32[]{:S(2)}) async-start(bf16[32,32,128]{2,1,0:T(8,128)(2,1)} %broadcast_in_dim.39), calls=%async_computation.3 | async-start | bytes 524288 | tf_op jit(solution)/shard_map/all_to_all | solution.py:445
  74.5 0.0 copy-start.3
  74.5 0.0 copy-start.4
  74.5 0.0 copy-start
  74.6 0.0 copy-start.1
  74.6 0.7 collective-permute-start.1
  75.3 0.0 collective-permute-done.1.passed_ref
  75.3 0.0 copy-start.2
  75.3 0.0 copy-done.5
  75.3 0.0 copy-done.6
  75.3 0.0 copy-done.3
  75.3 0.0 copy-done.4
  75.3 0.0 copy-done
  75.3 0.0 copy-done.1
  75.3 0.6 copy-done.2
  76.0 1.5 %finish.1 = (f32[512,128]{1,0:T(8,128)}, bf16[256,128]{1,0:T(8,128)(2,1)}) custom-call(bf16[32,64,128]{2,1,0:T(8,128)(2,1)S(1)} %all_to_all.20.recv_ref, bf16[64,128]{1,0:T(8,128)(2,1)S(1)} %collective-permute-done.1.passed_ref, f32[512,128]{1,0:T(8,128)S(1)} %copy-done.5, bf16[512,128]{1,0:T(8,128)(2,1)S(1)} %copy-done.6, s32[8,8]{1,0:T(8,128)S(1)} %bitcast.34, ...), custom_call_target="tpu_custom_call" | custom-call | flops 300000000 | bytes 2000000 | tf_op jit(solution)/shard_map/finish/pallas_call | solution.py:403
  77.5 6.0 %all-to-all-done.3 = bf16[32,32,128]{2,1,0:T(8,128)(2,1)S(1)} async-done(((bf16[32,32,128]{2,1,0:T(8,128)(2,1)}), bf16[32,32,128]{2,1,0:T(8,128)(2,1)S(1)}, u32[]{:S(2)}, u32[]{:S(2)}) %all-to-all-start.3) | async-done | bytes 262176 | tf_op jit(solution)/shard_map/all_to_all | solution.py:445
  83.5 0.8 unpack.1
  (6 shorter events, 0.1 us)
Async XLA Ops:
  2.5 2.6 %collective-permute-start = (bf16[64,128]{1,0:T(8,128)(2,1)}, bf16[64,128]{1,0:T(8,128)(2,1)S(1)}, u32[]{:S(2)}, u32[]{:S(2)}) collective-permute-start(bf16[64,128]{1,0:T(8,128)(2,1)} %faces.1), channel_id=1, source_target_pairs={{8,16},{24,32},{40,48},{56,64},{72,80},{88,96},{104,112},{120,128}... | collective-permute-start | bytes 49160 | tf_op jit(solution)/shard_map/ppermute | solution.py:442
  5.7 16.1 %all-to-all-start = ((bf16[16,32,128]{2,1,0:T(8,128)(2,1)}), bf16[16,32,128]{2,1,0:T(8,128)(2,1)S(1)}, u32[]{:S(2)}, u32[]{:S(2)}) async-start(bf16[16,32,128]{2,1,0:T(8,128)(2,1)} %bitcast_dynamic-update-slice_fusion), calls=%async_computation | async-start | bytes 262144 | tf_op jit(solution)/shard_map/all_to_all | solution.py:445
  21.8 0.7 copy-start.7
  69.0 6.3 %copy-start.5 = (f32[512,128]{1,0:T(8,128)S(1)}, f32[512,128]{1,0:T(8,128)}, u32[]{:S(2)}) copy-start(f32[512,128]{1,0:T(8,128)} %get-tuple-element.29.d_node_ref) | copy-start | bytes 786436
  69.0 6.3 %copy-start.6 = (bf16[512,128]{1,0:T(8,128)(2,1)S(1)}, bf16[512,128]{1,0:T(8,128)(2,1)}, u32[]{:S(2)}) copy-start(bf16[512,128]{1,0:T(8,128)(2,1)} %get-tuple-element.30.fresh_ref) | copy-start | bytes 393220
  69.0 14.5 %all-to-all-start.3 = ((bf16[32,32,128]{2,1,0:T(8,128)(2,1)}), bf16[32,32,128]{2,1,0:T(8,128)(2,1)S(1)}, u32[]{:S(2)}, u32[]{:S(2)}) async-start(bf16[32,32,128]{2,1,0:T(8,128)(2,1)} %broadcast_in_dim.39), calls=%async_computation.3 | async-start | bytes 524288 | tf_op jit(solution)/shard_map/all_to_all | solution.py:445
  74.5 0.8 copy-start.3
  74.5 0.8 copy-start.4
  74.5 0.8 copy-start
  74.6 0.8 copy-start.1
  74.6 0.7 collective-permute-start.1
  75.3 0.7 copy-start.2

commit v4 on v3

v4 whole, which is shorter than its diff:
```python
import functools
import math

import jax
import jax.numpy as jnp
from jax import lax
from jax.experimental import pallas as pl
from jax.experimental.pallas import tpu as pltpu
from jax.sharding import Mesh
from jax.sharding import PartitionSpec as P

NORM_EPSILON = 1e-05
F32 = jnp.float32
BF16 = jnp.bfloat16
MIB = 1024 * 1024

PAIR = ("y0", "sub")
PLANE = ("y1", "y0", "sub")
FIRST = 32
HEAD = 24
GRAD_ROWS = 1024


def mm(a, b):
    return lax.dot_general(a, b, (((1,), (0,)), ((), ())), preferred_element_type=F32)


def mm_nt(a, b):
    return lax.dot_general(a, b, (((1,), (1,)), ((), ())), preferred_element_type=F32)


def mm_tn(a, b):
    return lax.dot_general(a, b, (((0,), (0,)), ((), ())), preferred_element_type=F32)


def iota(shape, dim):
    return lax.broadcasted_iota(jnp.int32, shape, dim)


def onehot(mask):
    return jnp.where(mask, 1.0, 0.0).astype(BF16)


def two_parts(x):
    high = x.astype(BF16)
    low = (x - high.astype(F32)).astype(BF16)
    return high, low


def column_of(ids):
    a, b = ids.shape
    spread = jnp.broadcast_to(ids[:, None, :], (a, b, b))
    keep = iota((a, b, b), 1) == iota((a, b, b), 2)
    return jnp.sum(jnp.where(keep, spread, 0), axis=2, keepdims=True).reshape(a * b, 1)


def face_column(face_row, pick):
    spot = column_of(pick)
    shape = (spot.shape[0], face_row.shape[1])
    keep = spot == iota(shape, 1)
    return jnp.sum(jnp.where(keep, jnp.broadcast_to(face_row, shape), 0), axis=1, keepdims=True)


def onehot_rows(column, width):
    return onehot(column == iota((column.shape[0], width), 1))


def slab_in_plane():
    return lax.axis_index("y1") * lax.axis_size("y0") + lax.axis_index("y0")


def picked_rows(node, bound_ref, pick_ref, side):
    face_row = jnp.where(side == 0, bound_ref[0:1, :], bound_ref[1:2, :])
    return mm(onehot_rows(face_column(face_row, pick_ref[side]), node.shape[0]), node)


def face_kernel(node_ref, bound_ref, pick_ref, out_ref):
    out_ref[...] = picked_rows(node_ref[...], bound_ref, pick_ref, lax.axis_index("y0")).astype(BF16)


def send_kernel(count_ref, intra_ref, bound_ref, pick_ref, *refs):
    arrays = (len(refs) - 4) // 2
    far, near, sem = refs[:arrays], refs[arrays + 3 : -1], refs[-1]
    out_ref, count_out_ref, onward_ref = refs[arrays : arrays + 3]
    copies = [pltpu.make_async_copy(far[k], near[k], sem.at[k]) for k in range(arrays)]
    for copy in copies:
        copy.start()
    node_ref, second_ref, coarse_cot_ref = near[0:3]
    count_out_ref[...] = jnp.full(count_out_ref.shape, count_ref[0, 0], jnp.int32)
    slab = slab_in_plane()
    last = lax.axis_size("y1") * lax.axis_size("y0") - 1
    half_rows = onward_ref.shape[0] // 2
    for k, reader in ((0, last), (1, 0)):
        column = jnp.where(slab == reader, column_of(pick_ref[1 - k]), -1)
        onward_ref[half_rows * k : half_rows * (k + 1), :] = onehot_rows(column, 128)
    for copy in copies[0:3]:
        copy.wait()
    odd = lax.axis_index("y0")
    node = node_ref[...]
    cells, feature = node.shape
    peers, halo = intra_ref.shape
    coarse = coarse_cot_ref.shape[0]
    intra = mm(onehot_rows(column_of(intra_ref[...]), cells), node)
    half = 0.5 * coarse_cot_ref[...].astype(F32)
    pool_rows = 16 * peers
    pool = mm(onehot(second_ref[...] - cells == iota((pool_rows, coarse), 0)), half.astype(BF16))
    same = [
        intra.reshape(peers, halo, feature),
        jnp.zeros((peers, halo, feature), F32),
        pool.reshape(peers, 16, feature),
    ]
    other = [
        picked_rows(node, bound_ref, pick_ref, 1 - odd).reshape(peers, halo, feature),
        jnp.zeros((peers, FIRST - halo, feature), F32),
    ]
    out_ref[pl.ds(peers * odd, peers)] = jnp.concatenate(same, axis=1).astype(BF16)
    out_ref[pl.ds(peers * (1 - odd), peers)] = jnp.concatenate(other, axis=1).astype(BF16)
    for copy in copies[3:]:
        copy.wait()


def silu_parts(pre):
    sig = 0.5 * jnp.tanh(0.5 * pre) + 0.5
    act = (pre * sig).astype(BF16)
    slope = sig * (1.0 + pre * (1.0 - sig))
    return act, slope


def norm_forward(out, axis):
    centred = out - jnp.mean(out, axis=axis, keepdims=True)
    inv = lax.rsqrt(jnp.mean(centred * centred, axis=axis, keepdims=True) + NORM_EPSILON)
    return centred * inv, inv


def norm_backward(u, normed, inv, gain, axis):
    scaled = u * gain
    inner = (
        scaled
        - jnp.mean(scaled, axis=axis, keepdims=True)
        - normed * jnp.mean(scaled * normed, axis=axis, keepdims=True)
    )
    return inner * inv


def fold_lanes(x):
    total = x[:, 0:128]
    for k in range(1, x.shape[1] // 128):
        total = total + x[:, 128 * k : 128 * k + 128]
    return total


def column_block(row, width):
    block = jnp.broadcast_to(row, (128, 128)).T
    return jnp.concatenate([block] * (width // 128), axis=1)


def hot_columns(ids, rows):
    width = ids.shape[1]

    def spread(x):
        return jnp.broadcast_to(x.astype(F32), (16, width)).astype(BF16)

    tens, units = spread(ids & -16), spread(ids & 15)
    zero = jnp.zeros((16, width), BF16)
    base = jnp.where(units == iota((16, width), 0).astype(F32).astype(BF16), jnp.ones((16, width), BF16), zero)
    return jnp.concatenate(
        [jnp.where(tens == jnp.full((16, width), 16 * r, BF16), base, zero) for r in range(rows // 16)], axis=0
    )


def main_kernel(
    count_ref, recv_ref, node_ref, second_ref, coarse_cot_ref, src_ref, dst_ref, ew1_ref, eb1_ref, edges_ref,
    ew2_ref, eg_ref, nw1_ref, nb1_ref, nw2_ref, ng_ref, first_ref, match_ref, cot_ref,
    new_edges_out, d_edges_out, d_node_ref, fresh_ref, send_ref,
    new_edges_ref, d_edges_ref, table_ref, t2_ref, oht_ref, grads_ref, out_sem,
):
    cells, feature = node_ref.shape
    wide = table_ref.shape[0]
    oht_ref[0:wide, :] = hot_columns(src_ref[...], wide)
    oht_ref[wide:, :] = hot_columns(dst_ref[...], cells)
    slots = edges_ref.shape[0]
    peers = recv_ref.shape[0] // 2
    count = count_ref[0:1, 0:1]
    node = node_ref[...]
    odd = lax.axis_index("y0")
    same = recv_ref[pl.ds(peers * odd, peers)]
    near = same.astype(F32)
    other = recv_ref[pl.ds(peers * (1 - odd), peers)].astype(F32)[:, 0:8, :]
    passed = near[:, 8:16, :]
    kinds = [near[:, 0:8, :], jnp.where(odd == 0, passed, other), jnp.where(odd == 0, other, passed)]
    halo_rows = 3 * 8 * peers
    table_ref[0:cells, :] = node
    halo = jnp.concatenate(
        [rows.reshape(8 * peers, feature) for rows in kinds]
        + [jnp.zeros((wide - cells - halo_rows, feature), F32)],
        axis=0,
    )
    table_ref[cells:wide, :] = halo.astype(BF16)
    ew1_edge_t = ew1_ref[0:feature, :].T
    ew1_src = ew1_ref[feature : 2 * feature, :]
    ew1_dst = ew1_ref[2 * feature : 3 * feature, :]
    high, low = two_parts(mm_nt(ew1_src.T, table_ref[...]))
    t2_ref[0:feature, 0:wide] = high
    t2_ref[feature:, 0:wide] = low
    high, low = two_parts(mm_nt(ew1_dst.T, node) + column_block(eb1_ref[...], cells))
    t2_ref[0:feature, wide:] = high
    t2_ref[feature:, wide:] = low
    ew2 = ew2_ref[...]
    eg = column_block(eg_ref[...], slots)
    live_column = iota((feature, slots), 1) < count
    live_row = iota((slots, feature), 0) < count

    both = mm(t2_ref[...], oht_ref[...])
    pre = both[0:feature] + both[feature:] + mm_nt(ew1_edge_t, edges_ref[...])
    edge_act, edge_slope = silu_parts(pre)
    edge_normed, edge_inv = norm_forward(mm(ew2.T, edge_act), 0)
    message = jnp.where(live_column, edge_normed * eg, 0.0)
    new_edges = jnp.where(live_row, edges_ref[...].astype(F32) + message.T, 0.0)
    new_edges_ref[...] = new_edges.astype(BF16)
    edges_copy = pltpu.make_async_copy(new_edges_ref, new_edges_out, out_sem.at[0])
    edges_copy.start()
    both = mm_nt(oht_ref[wide:, :], jnp.concatenate(two_parts(message), axis=0))
    aggregate = (both[:, 0:feature] + both[:, feature:]).astype(BF16)

    nw1_node = nw1_ref[0:feature, :]
    nw1_agg = nw1_ref[feature:, :]
    pre = mm(node, nw1_node) + mm(aggregate, nw1_agg) + nb1_ref[...]
    act, slope = silu_parts(pre)
    nw2 = nw2_ref[...]
    ng = ng_ref[...]
    normed, inv = norm_forward(mm(act, nw2), 1)
    fresh = (node.astype(F32) + normed * ng).astype(BF16)
    fresh_ref[...] = fresh

    coarse = coarse_cot_ref.shape[0]
    half = (0.5 * coarse_cot_ref[...].astype(F32)).astype(BF16)
    cell_row = iota((cells, coarse), 0)
    pooled = onehot((first_ref[...] == cell_row) | (second_ref[...] == cell_row))
    returned = same[:, 16:32, :].reshape(16 * peers, feature)
    hot_match = onehot_rows(column_of(match_ref[...]), cells)
    d_fresh = mm(pooled, half) + mm_tn(hot_match, returned)
    match_rows = mm(hot_match, fresh)

    d_out = norm_backward(d_fresh, normed, inv, ng, 1)
    grads_ref[899:900, :] = jnp.sum(d_fresh * normed, axis=0, keepdims=True)
    d_out_half = d_out.astype(BF16)
    grads_ref[768:896, :] = mm_tn(act, d_out_half)
    d_pre = mm_nt(d_out_half, nw2) * slope
    grads_ref[898:899, :] = jnp.sum(d_pre, axis=0, keepdims=True)
    d_pre_half = d_pre.astype(BF16)
    grads_ref[512:640, :] = mm_tn(node, d_pre_half)
    grads_ref[640:768, :] = mm_tn(aggregate, d_pre_half)
    d_node_ref[...] = d_fresh + mm_nt(d_pre_half, nw1_node)
    high, low = two_parts(mm_nt(nw1_agg, d_pre_half))

    both = mm(jnp.concatenate([high, low], axis=0), oht_ref[wide:, :])
    cot = jnp.where(live_row, cot_ref[...].astype(F32), 0.0)
    u = jnp.where(live_column, cot.T + (both[0:feature] + both[feature:]), 0.0)
    d_out_half = norm_backward(u, edge_normed, edge_inv, eg, 0).astype(BF16)
    d_gain = fold_lanes(u * edge_normed)
    d_pre = mm(ew2, d_out_half) * edge_slope
    d_pre_half = d_pre.astype(BF16)
    d_edges_ref[...] = (cot + mm_tn(d_pre_half, ew1_edge_t)).astype(BF16)
    d_edges_copy = pltpu.make_async_copy(d_edges_ref, d_edges_out, out_sem.at[1])
    d_edges_copy.start()
    scattered = mm_nt(oht_ref[...], d_pre_half)

    grads_ref[0:128, :] = mm(d_pre_half, edges_ref[...]).T
    grads_ref[384:512, :] = mm_nt(edge_act, d_out_half)
    grads_ref[896:897, :] = jnp.sum(fold_lanes(d_pre).T, axis=0, keepdims=True)
    grads_ref[897:898, :] = jnp.sum(d_gain.T, axis=0, keepdims=True)
    grads_ref[900:, :] = jnp.zeros_like(grads_ref[900:, :])
    high, low = two_parts(scattered[0:wide])
    table = table_ref[...]
    grads_ref[128:256, :] = mm_tn(table, high) + mm_tn(table, low)
    d_table = mm_nt(high, ew1_src) + mm_nt(low, ew1_src)
    high, low = two_parts(scattered[wide:])
    grads_ref[256:384, :] = mm_tn(node, high) + mm_tn(node, low)
    d_node_ref[...] += d_table[0:cells, :] + (mm_nt(high, ew1_dst) + mm_nt(low, ew1_dst))
    kinds = [
        d_table[cells + 8 * peers * k : cells + 8 * peers * (k + 1), :].reshape(peers, 8, feature)
        for k in range(3)
    ]
    slab = slab_in_plane()
    slabs = send_ref.shape[0] // peers
    share = GRAD_ROWS // (slabs * peers)
    blank = jnp.zeros((peers, 8, feature), F32)
    first_plane, last_plane = slab == 0, slab == slabs - 1
    heads = [
        [kinds[0], match_rows.reshape(peers, 16, feature)],
        [kinds[2], jnp.where(last_plane, kinds[2], 0.0), blank],
    ]
    heads += [[blank, blank, blank]] * (slabs - 3)
    heads += [[kinds[1], jnp.where(first_plane, kinds[1], 0.0), blank]]
    for step, head in enumerate(heads):
        to = lax.rem(slab + step, slabs)
        grads = grads_ref[pl.ds(pl.multiple_of(to * (peers * share), 8), peers * share), :]
        block = jnp.concatenate(head + [grads.reshape(peers, share, feature)], axis=1)
        send_ref[pl.ds(peers * to, peers)] = block.astype(BF16)
    edges_copy.wait()
    d_edges_copy.wait()


def unpack(recv_ref, w1_ref, w2_ref, nw1_ref, nw2_ref, b1_ref, g_ref, nb1_ref, ng_ref):
    start = 0
    for out_ref in (w1_ref, w2_ref, nw1_ref, nw2_ref):
        rows = out_ref.shape[0]
        out_ref[...] = recv_ref[start : start + rows, :].astype(F32)
        start += rows
    tail = recv_ref[start : start + 16, :].astype(F32)
    for k, out_ref in enumerate((b1_ref, g_ref, nb1_ref, ng_ref)):
        out_ref[...] = tail[k : k + 1, :]


def finish_kernel(
    recv_ref, planes_ref, d_node_ref, fresh_ref, intra_ref, bound_ref,
    pick_ref, first_ref, second_ref, grads_ref, d_out_ref, coarse_ref, *weight_refs,
):
    unpack(grads_ref, *weight_refs)
    peers = intra_ref.shape[0]
    slabs = recv_ref.shape[0] // peers
    planes = planes_ref.shape[0]
    cells, feature = d_node_ref.shape
    slab = slab_in_plane()
    plane = lax.axis_index("z")

    def block_of(y):
        return recv_ref[pl.ds(peers * y, peers)].astype(F32)

    def gradients(block):
        return block[:, 0:8, :].reshape(8 * peers, feature).astype(BF16)

    same = block_of(slab)
    hot = onehot_rows(column_of(intra_ref[...]), cells)
    total = mm_tn(hot, gradients(same))
    faces = bound_ref.shape[1]
    first_row = planes_ref.shape[1] - faces
    for k, step, edge in ((0, -1, slab == 0), (1, 1, slab == slabs - 1)):
        face_row = bound_ref[k : k + 1, :]
        direct = gradients(block_of(lax.rem(slab + step + slabs, slabs)))
        direct = jnp.where(edge, jnp.zeros_like(direct), direct)
        total = total + mm_tn(onehot_rows(face_column(face_row, pick_ref[k]), cells), direct)
        far = jnp.clip(plane + step, 0, planes - 1)
        passed = planes_ref[far, first_row:, :]
        passed = jnp.where(edge & (far != plane), passed, jnp.zeros_like(passed))
        total = total + mm_tn(onehot_rows(column_of(face_row), cells), passed)
    d_out_ref[...] = d_node_ref[...] + total
    partners = same[:, 8:24, :].reshape(16 * peers, feature).astype(BF16)
    coarse = coarse_ref.shape[0]
    cell_row = iota((cells, coarse), 0)
    near = onehot((first_ref[...] == cell_row) | (second_ref[...] == cell_row))
    far = onehot(second_ref[...] - cells == iota((16 * peers, coarse), 0))
    coarse_ref[...] = (0.5 * (mm_tn(near, fresh_ref[...]) + mm_tn(far, partners))).astype(BF16)


def call(kernel, out_shape, *args, scratch=(), smem=(), hbm=(), hbm_out=(), held=(), name=None, cost=None, mib=8):
    def space(i, far):
        return pltpu.HBM if i in far else pltpu.VMEM

    one = not isinstance(out_shape, tuple)
    outs = [pl.BlockSpec(memory_space=space(i, hbm_out)) for i in range(1 if one else len(out_shape))]
    args = [pltpu.with_memory_space_constraint(x, pltpu.HBM) if i in hbm or i in held else x for i, x in enumerate(args)]
    return pl.pallas_call(
        kernel,
        out_shape=out_shape,
        in_specs=[
            pl.BlockSpec(memory_space=pltpu.SMEM if i in smem else space(i, hbm)) for i in range(len(args))
        ],
        out_specs=outs[0] if one else tuple(outs),
        scratch_shapes=list(scratch),
        compiler_params=pltpu.CompilerParams(vmem_limit_bytes=mib * MIB),
        name=name,
        cost_estimate=cost,
    )(*args)


def shape_of(shape, dtype):
    return jax.ShapeDtypeStruct(shape, dtype)


def per_device(
    slabs, node, edges, edge_src, edge_dst, edge_count, intra_idx, bound_idx, cross_pick,
    match_send, pool_first, pool_second, edge_w1, edge_b1, edge_w2, edge_gain,
    node_w1, node_b1, node_w2, node_gain, edge_cot, coarse_cot,
):
    node, edges, edge_cot, coarse_cot = node[0, 0], edges[0, 0], edge_cot[0, 0], coarse_cot[0, 0]
    intra, bound, pick, match = intra_idx[0, 0], bound_idx[0, 0], cross_pick[0], match_send[0, 0]
    first, second = pool_first[0], pool_second[0]
    src, dst = edge_src[0], edge_dst[0]
    cells, feature = node.shape
    slots = edges.shape[0]
    coarse = coarse_cot.shape[0]
    peers = lax.axis_size("sub")
    planes = lax.axis_size("z")
    in_plane = slabs // planes
    dom = ("z", "y1", "y0")
    face = shape_of((8 * peers, feature), BF16)
    wide = -(-(cells + 24 * peers) // 256) * 256

    def swap(rows):
        pairs = [(i - 1, i) for i in range(2, slabs, 2)]
        return lax.ppermute(rows, dom, pairs + [(j, i) for i, j in pairs])

    def exchange(blocks, axes):
        return lax.all_to_all(blocks, axes, split_axis=0, concat_axis=0, tiled=True)

    passed = swap(call(face_kernel, face, node, bound, pick, held=range(3), name="faces"))
    far = (
        node, second, coarse_cot, src, dst, edge_w1, edge_b1[None], edges, edge_w2, edge_gain[None],
        node_w1, node_b1[None], node_w2, node_gain[None], first, match, edge_cot, intra, bound, pick,
    )
    sent, count, onward_pick, *near = call(
        send_kernel,
        (shape_of((2 * peers, FIRST, feature), BF16), shape_of((8, 128), jnp.int32), shape_of((16 * peers, 128), BF16))
        + tuple(shape_of(x.shape, x.dtype) for x in far),
        edge_count, intra, bound, pick, *far,
        smem=(0,), held=range(1, 4), hbm=range(4, 4 + len(far)),
        scratch=[pltpu.SemaphoreType.DMA((len(far),))],
        name="send",
        cost=pl.CostEstimate(flops=60_000_000, bytes_accessed=400_000, transcendentals=0),
    )
    passed = passed.reshape(peers, 8, feature)
    passed = jnp.concatenate([passed, passed], axis=0)
    sent = jnp.concatenate([sent[:, 0:8], passed, sent[:, 16:]], axis=1)
    received = exchange(sent, PAIR)

    new_edges, d_edges, d_node, fresh, sent = call(
        main_kernel,
        (
            shape_of((slots, feature), BF16),
            shape_of((slots, feature), BF16),
            shape_of((cells, feature), F32),
            shape_of((cells, feature), BF16),
            shape_of((in_plane * peers, HEAD + GRAD_ROWS // (in_plane * peers), feature), BF16),
        ),
        count, received, *near[:-3],
        hbm_out=(0, 1),
        scratch=[
            pltpu.VMEM((slots, feature), BF16),
            pltpu.VMEM((slots, feature), BF16),
            pltpu.VMEM((wide, feature), BF16),
            pltpu.VMEM((2 * feature, wide + cells), BF16),
            pltpu.VMEM((wide + cells, slots), BF16),
            pltpu.VMEM((GRAD_ROWS, feature), F32),
            pltpu.SemaphoreType.DMA((2,)),
        ],
        name="layer",
        mib=28,
    )
    received = exchange(sent, PLANE)
    scale = 1.0 / math.sqrt(slabs * peers * slots)

    def total(blocks):
        return jnp.sum(blocks.astype(F32), axis=0)

    def copies(rows, count):
        return jnp.broadcast_to(rows, (count,) + rows.shape)

    ends = jnp.concatenate([received[0:peers, 8:16], received[-peers:, 8:16]], axis=0)
    onward = mm_tn(onward_pick, ends.reshape(16 * peers, feature))[0 : bound.shape[1]]
    rows = jnp.concatenate([total(received[:, HEAD:]), onward], axis=0).astype(BF16)
    by_plane = exchange(copies(rows, planes), "z")
    share = rows.shape[0] - onward.shape[0]
    rows = (total(by_plane[:, 0:share]) * scale).astype(BF16)
    grads = exchange(copies(rows, in_plane * peers), PLANE)
    row = shape_of((1, feature), F32)
    d_node, coarse_out, w1, w2, nw1, nw2, b1, g, nb1, ng = call(
        finish_kernel,
        (
            shape_of((cells, feature), F32),
            shape_of((coarse, feature), BF16),
            shape_of((3 * feature, feature), F32),
            shape_of((feature, feature), F32),
            shape_of((2 * feature, feature), F32),
            shape_of((feature, feature), F32),
            row, row, row, row,
        ),
        received, by_plane, d_node, fresh, *near[-3:], near[14], near[1], grads.reshape(GRAD_ROWS, feature),
        name="finish",
    )
    return (
        new_edges[None, None], coarse_out[None, None], d_node[None, None], d_edges[None, None],
        w1, b1[0], w2, g[0], nw1, nb1[0], nw2, ng[0],
    )


def solution(mesh):
    slabs, peers = mesh.shape["dom"], mesh.shape["sub"]
    devices = mesh.devices.reshape(slabs // 4, 2, 2, peers)
    dom = ("z", "y1", "y0")
    inner = Mesh(devices, dom + ("sub",))
    four, three = P(dom, "sub", None, None), P(dom, "sub", None)
    return jax.shard_map(
        functools.partial(per_device, slabs),
        mesh=inner,
        in_specs=(
            four, four, three, three, P(dom, "sub"), four, four, P("sub", None, None, None),
            four, three, three, P(), P(), P(), P(), P(), P(), P(), P(), four, four,
        ),
        out_specs=(four, four, four, four) + (P(),) * 8,
        check_vma=False,
    )
```

time: 84.9 us -> 79.7 us (0.939)
  blocking collectives: 34.3 us -> 62.3 us
  starting transfers between devices: 16.9 us -> 0.66 us
  waiting for transfers between devices: 11.5 us -> 0.01 us
  Pallas kernels: 17.4 us -> 14.7 us
  local copies, waits for them, and re-layouts: 2.68 us -> 0.07 us
    all_to_all x2 -> x4, blocking collectives: 34.3 us -> 62.3 us  [exchange(): return lax.all_to_all(blocks, axes, split_axis=0, concat_axis=0, tiled=True)]
    all_to_all x2 -> x0, starting transfers between devices: 15.6 us -> none  [exchange(): return lax.all_to_all(blocks, axes, split_axis=0, concat_axis=0, tiled=True)]
    all_to_all x2 -> x0, waiting for transfers between devices: 11.5 us -> none  [exchange(): return lax.all_to_all(blocks, axes, split_axis=0, concat_axis=0, tiled=True)]
    pallas_call x5 -> x4, Pallas kernels: 17.4 us -> 14.7 us  [call(): pl.pallas_call(kernel, out_shape=out_shape, in_specs=[pl.BlockSpec(memory...]
    unnamed x16 -> x0, local copies, waits for them, and re-layouts: 1.3 us -> none
  transfers between devices with their start and end apart: 4 -> 1, of which waited for: 2 -> 0; matrix products, arithmetic and copies ran while one was open for 0% -> 0% of each run, Pallas kernels for 2% -> 0%
where the time goes in v4:
time: 79.7 us; the launch traced here: 79.4 us
  blocking collectives  62.3 us (78%)
  Pallas kernels  14.7 us (18%)
  between operations  1.4 us (2%)
    all_to_all x4, blocking collectives, exchange(): return lax.all_to_all(blocks, axes, split_axis=0, concat_axis=0, tiled=True)  62.3 us
    pallas_call x4, Pallas kernels, call(): pl.pallas_call(kernel, out_shape=out_shape, in_specs=[pl.BlockSpec(memory...  14.7 us
  transfers between devices with their start and end apart: 1, of which 0 were waited for; matrix products, arithmetic and copies ran while one was open for 0% of the time, Pallas kernels for 0%

profile of v4, /device:TPU:1, one launch (start us, length us, event | category | flops | bytes accessed | tf_op | source)
XLA Modules:
  0.0 79.4 jit_solution(16285121156070426610)
XLA Ops:
  0.6 1.2 %faces.1 = bf16[64,128]{1,0:T(8,128)(2,1)S(1)} custom-call(bf16[512,128]{1,0:T(8,128)(2,1)} %bitcast.33, s32[2,16]{1,0:T(2,128)} %bitcast.42, s32[2,8,8]{2,1,0:T(8,128)} %bitcast.35), custom_call_target="tpu_custom_call" | custom-call | tf_op jit(solution)/shard_map/faces/pallas_call | solution.py:363
  1.9 0.7 collective-permute-start
  3.2 2.5 %send.1 = (bf16[16,32,128]{2,1,0:T(8,128)(2,1)S(1)}, s32[8,128]{1,0:T(8,128)S(1)}, bf16[128,128]{1,0:T(8,128)(2,1)S(1)}, bf16[512,128]{1,0:T(8,128)(2,1)S(1)}, s...) custom-call(s32[1,1]{1,0:T(1,128)S(6)} %copy.33.count_ref, ...), custom_call_target="tpu_custom_call" | custom-call | flops 60000000 | bytes 400000 | tf_op jit(solution)/shard_map/send/pallas_call | solution.py:363
  5.8 0.0 collective-permute-done
  5.8 15.5 %all_to_all.20.recv_ref = bf16[16,32,128]{2,1,0:T(8,128)(2,1)S(1)} all-to-all(bf16[16,32,128]{2,1,0:T(8,128)(2,1)S(1)} %pad_maximum_fusion), channel_id=1, replica_groups=mesh['z'=8,'y1'=2,'y0'=2,'sub'=8] {'y0','sub'}, dimensions={0} | all-to-all | bytes 262144 | tf_op jit(solution)/shard_map/all_to_all | solution.py:405
  21.3 9.3 %layer.1 = (bf16[2048,128]{1,0:T(8,128)(2,1)}, bf16[2048,128]{1,0:T(8,128)(2,1)}, f32[512,128]{1,0:T(8,128)S(1)}, bf16[512,128]{1,0:T(8,128)(2,1)S(1)}, bf16[32,56,128]{2,1,0:T(8,128)(2,1)S(1)}) custom-call(s32[8,128]{1,0:T(8,128)S(1)} %get-tuple-element.50.count_ref, bf16[16,32,128]{2,1,0:T(8,128)(2,1)S(1)} %all_to_all.20.recv_ref, ...), custom_call_target="tpu_custom_call" | custom-call | tf_op jit(solution)/shard_map/layer/pallas_call | solution.py:363
  30.7 17.1 %all_to_all.21.recv_ref = bf16[32,56,128]{2,1,0:T(8,128)(2,1)S(1)} all-to-all(bf16[32,56,128]{2,1,0:T(8,128)(2,1)S(1)} %get-tuple-element.70), channel_id=1, replica_groups=mesh['z'=8,'y1'=2,'y0'=2,'sub'=8] {'y1','y0','sub'}, dimensions={0} | all-to-all | bytes 917504 | tf_op jit(solution)/shard_map/all_to_all | solution.py:405
  47.8 0.2 fusion
  48.0 0.1 slice_reduce_fusion
  48.1 15.4 %all_to_all.22.planes_ref = bf16[8,48,128]{2,1,0:T(8,128)(2,1)S(1)} all-to-all(bf16[8,48,128]{2,1,0:T(8,128)(2,1)S(1)} %broadcast_in_dim.35), channel_id=1, replica_groups=mesh['z'=8,'y1'=2,'y0'=2,'sub'=8] {'z'}, dimensions={0} | all-to-all | bytes 196608 | tf_op jit(solution)/shard_map/all_to_all | solution.py:405
  63.6 14.2 %all_to_all.23 = bf16[32,32,128]{2,1,0:T(8,128)(2,1)S(1)} all-to-all(bf16[32,32,128]{2,1,0:T(8,128)(2,1)S(1)} %broadcast_in_dim.36), channel_id=1, replica_groups=mesh['z'=8,'y1'=2,'y0'=2,'sub'=8] {'y1','y0','sub'}, dimensions={0} | all-to-all | bytes 524288 | tf_op jit(solution)/shard_map/all_to_all | solution.py:405
  77.8 1.6 %finish.1 = (f32[512,128]{1,0:T(8,128)}, bf16[256,128]{1,0:T(8,128)(2,1)}, f32[384,128]{1,0:T(8,128)}, f32[128,128]{1,0:T(8,128)}, f32[256,128]{1,0:T(8,128)}, /...) custom-call(bf16[32,56,128]{2,1,0:T(8,128)(2,1)S(1)} %all_to_all.21.recv_re, ...), custom_call_target="tpu_custom_call" | custom-call | tf_op jit(solution)/shard_map/finish/pallas_call | solution.py:363
  (10 shorter events, 0.1 us)
Async XLA Ops:
  1.9 3.9 %collective-permute-start = (bf16[64,128]{1,0:T(8,128)(2,1)S(1)}, bf16[64,128]{1,0:T(8,128)(2,1)S(1)}, u32[]{:S(2)}, u32[]{:S(2)}) collective-permute-start(bf16[64,128]{1,0:T(8,128)(2,1)S(1)} %faces.1), channel_id=1, source_target_pairs={{8,16},{24,32},{40,48},{56,64},{72,80},{88,96},{104,112},{120,128}... | collective-permute-start | bytes 49160 | tf_op jit(solution)/shard_map/ppermute | solution.py:402

commit v5 on v4

--- a/solution.py
+++ b/solution.py
@@ -172,7 +172,7 @@
     count_ref, recv_ref, node_ref, second_ref, coarse_cot_ref, src_ref, dst_ref, ew1_ref, eb1_ref, edges_ref,
     ew2_ref, eg_ref, nw1_ref, nb1_ref, nw2_ref, ng_ref, first_ref, match_ref, cot_ref,
     new_edges_out, d_edges_out, d_node_ref, fresh_ref, send_ref,
-    new_edges_ref, d_edges_ref, table_ref, t2_ref, oht_ref, grads_ref, out_sem,
+    new_edges_ref, d_edges_ref, table_ref, ends_ref, oht_ref, grads_ref, out_sem,
 ):
     cells, feature = node_ref.shape
     wide = table_ref.shape[0]
@@ -199,19 +199,15 @@
     ew1_edge_t = ew1_ref[0:feature, :].T
     ew1_src = ew1_ref[feature : 2 * feature, :]
     ew1_dst = ew1_ref[2 * feature : 3 * feature, :]
-    high, low = two_parts(mm_nt(ew1_src.T, table_ref[...]))
-    t2_ref[0:feature, 0:wide] = high
-    t2_ref[feature:, 0:wide] = low
-    high, low = two_parts(mm_nt(ew1_dst.T, node) + column_block(eb1_ref[...], cells))
-    t2_ref[0:feature, wide:] = high
-    t2_ref[feature:, wide:] = low
     ew2 = ew2_ref[...]
     eg = column_block(eg_ref[...], slots)
     live_column = iota((feature, slots), 1) < count
     live_row = iota((slots, feature), 0) < count
 
-    both = mm(t2_ref[...], oht_ref[...])
-    pre = both[0:feature] + both[feature:] + mm_nt(ew1_edge_t, edges_ref[...])
+    ends_ref[0:feature, :] = mm(table_ref[...].T, oht_ref[0:wide, :]).astype(BF16)
+    ends_ref[feature:, :] = mm(node.T, oht_ref[wide:, :]).astype(BF16)
+    pre = mm(ew1_ref[feature:, :].T, ends_ref[...]) + mm_nt(ew1_edge_t, edges_ref[...])
+    pre = pre + column_block(eb1_ref[...], slots)
     edge_act, edge_slope = silu_parts(pre)
     edge_normed, edge_inv = norm_forward(mm(ew2.T, edge_act), 0)
     message = jnp.where(live_column, edge_normed * eg, 0.0)
@@ -219,8 +215,8 @@
     new_edges_ref[...] = new_edges.astype(BF16)
     edges_copy = pltpu.make_async_copy(new_edges_ref, new_edges_out, out_sem.at[0])
     edges_copy.start()
-    both = mm_nt(oht_ref[wide:, :], jnp.concatenate(two_parts(message), axis=0))
-    aggregate = (both[:, 0:feature] + both[:, feature:]).astype(BF16)
+    both = mm_nt(jnp.concatenate(two_parts(message), axis=0), oht_ref[wide:, :])
+    aggregate = (both[0:feature] + both[feature:]).T.astype(BF16)
 
     nw1_node = nw1_ref[0:feature, :]
     nw1_agg = nw1_ref[feature:, :]
@@ -251,11 +247,10 @@
     grads_ref[512:640, :] = mm_tn(node, d_pre_half)
     grads_ref[640:768, :] = mm_tn(aggregate, d_pre_half)
     d_node_ref[...] = d_fresh + mm_nt(d_pre_half, nw1_node)
-    high, low = two_parts(mm_nt(nw1_agg, d_pre_half))
-
-    both = mm(jnp.concatenate([high, low], axis=0), oht_ref[wide:, :])
+    d_aggregate = mm_nt(nw1_agg, d_pre_half).astype(BF16)
+
     cot = jnp.where(live_row, cot_ref[...].astype(F32), 0.0)
-    u = jnp.where(live_column, cot.T + (both[0:feature] + both[feature:]), 0.0)
+    u = jnp.where(live_column, cot.T + mm(d_aggregate, oht_ref[wide:, :]), 0.0)
     d_out_half = norm_backward(u, edge_normed, edge_inv, eg, 0).astype(BF16)
     d_gain = fold_lanes(u * edge_normed)
     d_pre = mm(ew2, d_out_half) * edge_slope
@@ -263,20 +258,17 @@
     d_edges_ref[...] = (cot + mm_tn(d_pre_half, ew1_edge_t)).astype(BF16)
     d_edges_copy = pltpu.make_async_copy(d_edges_ref, d_edges_out, out_sem.at[1])
     d_edges_copy.start()
-    scattered = mm_nt(oht_ref[...], d_pre_half)
+    scattered = mm_nt(d_pre_half, oht_ref[...]).astype(BF16)
+    d_table = mm(ew1_src, scattered[:, 0:wide]).T
+    d_target = mm(ew1_dst, scattered[:, wide:]).T
+    d_node_ref[...] += d_table[0:cells, :] + d_target
 
     grads_ref[0:128, :] = mm(d_pre_half, edges_ref[...]).T
     grads_ref[384:512, :] = mm_nt(edge_act, d_out_half)
     grads_ref[896:897, :] = jnp.sum(fold_lanes(d_pre).T, axis=0, keepdims=True)
     grads_ref[897:898, :] = jnp.sum(d_gain.T, axis=0, keepdims=True)
     grads_ref[900:, :] = jnp.zeros_like(grads_ref[900:, :])
-    high, low = two_parts(scattered[0:wide])
-    table = table_ref[...]
-    grads_ref[128:256, :] = mm_tn(table, high) + mm_tn(table, low)
-    d_table = mm_nt(high, ew1_src) + mm_nt(low, ew1_src)
-    high, low = two_parts(scattered[wide:])
-    grads_ref[256:384, :] = mm_tn(node, high) + mm_tn(node, low)
-    d_node_ref[...] += d_table[0:cells, :] + (mm_nt(high, ew1_dst) + mm_nt(low, ew1_dst))
+    grads_ref[128:384, :] = mm_nt(d_pre_half, ends_ref[...]).T
     kinds = [
         d_table[cells + 8 * peers * k : cells + 8 * peers * (k + 1), :].reshape(peers, 8, feature)
         for k in range(3)
@@ -439,7 +431,7 @@
             pltpu.VMEM((slots, feature), BF16),
             pltpu.VMEM((slots, feature), BF16),
             pltpu.VMEM((wide, feature), BF16),
-            pltpu.VMEM((2 * feature, wide + cells), BF16),
+            pltpu.VMEM((2 * feature, slots), BF16),
             pltpu.VMEM((wide + cells, slots), BF16),
             pltpu.VMEM((GRAD_ROWS, feature), F32),
             pltpu.SemaphoreType.DMA((2,)),

time: 79.7 us -> 77.8 us (0.976)
  Pallas kernels: 14.7 us -> 12.8 us
    pallas_call x4, Pallas kernels: 14.7 us -> 12.8 us  [call(): pl.pallas_call(kernel, out_shape=out_shape, in_specs=[pl.BlockSpec(memory...]
where the time goes in v5:
time: 77.8 us; the launch traced here: 77.5 us
  blocking collectives  62.3 us (80%)
  Pallas kernels  12.8 us (16%)
  between operations  1.4 us (2%)
    all_to_all x4, blocking collectives, exchange(): return lax.all_to_all(blocks, axes, split_axis=0, concat_axis=0, tiled=True)  62.3 us
    pallas_call x4, Pallas kernels, call(): pl.pallas_call(kernel, out_shape=out_shape, in_specs=[pl.BlockSpec(memory...  12.8 us
  transfers between devices with their start and end apart: 1, of which 0 were waited for; matrix products, arithmetic and copies ran while one was open for 0% of the time, Pallas kernels for 0%

profile of v5, /device:TPU:1, one launch (start us, length us, event | category | flops | bytes accessed | tf_op | source)
XLA Modules:
  0.0 77.5 jit_solution(15444493889367848693)
XLA Ops:
  0.6 1.2 %faces.1 = bf16[64,128]{1,0:T(8,128)(2,1)S(1)} custom-call(bf16[512,128]{1,0:T(8,128)(2,1)} %bitcast.33, s32[2,16]{1,0:T(2,128)} %bitcast.42, s32[2,8,8]{2,1,0:T(8,128)} %bitcast.35), custom_call_target="tpu_custom_call" | custom-call | tf_op jit(solution)/shard_map/faces/pallas_call | solution.py:355
  1.9 0.7 collective-permute-start
  3.2 2.5 %send.1 = (bf16[16,32,128]{2,1,0:T(8,128)(2,1)S(1)}, s32[8,128]{1,0:T(8,128)S(1)}, bf16[128,128]{1,0:T(8,128)(2,1)S(1)}, bf16[512,128]{1,0:T(8,128)(2,1)S(1)}, s...) custom-call(s32[1,1]{1,0:T(1,128)S(6)} %copy.33.count_ref, ...), custom_call_target="tpu_custom_call" | custom-call | flops 60000000 | bytes 400000 | tf_op jit(solution)/shard_map/send/pallas_call | solution.py:355
  5.8 0.0 collective-permute-done
  5.8 15.5 %all_to_all.20.recv_ref = bf16[16,32,128]{2,1,0:T(8,128)(2,1)S(1)} all-to-all(bf16[16,32,128]{2,1,0:T(8,128)(2,1)S(1)} %pad_maximum_fusion), channel_id=1, replica_groups=mesh['z'=8,'y1'=2,'y0'=2,'sub'=8] {'y0','sub'}, dimensions={0} | all-to-all | bytes 262144 | tf_op jit(solution)/shard_map/all_to_all | solution.py:397
  21.3 7.5 %layer.1 = (bf16[2048,128]{1,0:T(8,128)(2,1)}, bf16[2048,128]{1,0:T(8,128)(2,1)}, f32[512,128]{1,0:T(8,128)S(1)}, bf16[512,128]{1,0:T(8,128)(2,1)S(1)}, bf16[32,56,128]{2,1,0:T(8,128)(2,1)S(1)}) custom-call(s32[8,128]{1,0:T(8,128)S(1)} %get-tuple-element.50.count_ref, bf16[16,32,128]{2,1,0:T(8,128)(2,1)S(1)} %all_to_all.20.recv_ref, ...), custom_call_target="tpu_custom_call" | custom-call | tf_op jit(solution)/shard_map/layer/pallas_call | solution.py:355
  28.8 17.1 %all_to_all.21.recv_ref = bf16[32,56,128]{2,1,0:T(8,128)(2,1)S(1)} all-to-all(bf16[32,56,128]{2,1,0:T(8,128)(2,1)S(1)} %get-tuple-element.70), channel_id=1, replica_groups=mesh['z'=8,'y1'=2,'y0'=2,'sub'=8] {'y1','y0','sub'}, dimensions={0} | all-to-all | bytes 917504 | tf_op jit(solution)/shard_map/all_to_all | solution.py:397
  45.9 0.2 fusion
  46.1 0.1 slice_reduce_fusion
  46.2 15.4 %all_to_all.22.planes_ref = bf16[8,48,128]{2,1,0:T(8,128)(2,1)S(1)} all-to-all(bf16[8,48,128]{2,1,0:T(8,128)(2,1)S(1)} %broadcast_in_dim.35), channel_id=1, replica_groups=mesh['z'=8,'y1'=2,'y0'=2,'sub'=8] {'z'}, dimensions={0} | all-to-all | bytes 196608 | tf_op jit(solution)/shard_map/all_to_all | solution.py:397
  61.7 14.2 %all_to_all.23 = bf16[32,32,128]{2,1,0:T(8,128)(2,1)S(1)} all-to-all(bf16[32,32,128]{2,1,0:T(8,128)(2,1)S(1)} %broadcast_in_dim.36), channel_id=1, replica_groups=mesh['z'=8,'y1'=2,'y0'=2,'sub'=8] {'y1','y0','sub'}, dimensions={0} | all-to-all | bytes 524288 | tf_op jit(solution)/shard_map/all_to_all | solution.py:397
  75.9 1.6 %finish.1 = (f32[512,128]{1,0:T(8,128)}, bf16[256,128]{1,0:T(8,128)(2,1)}, f32[384,128]{1,0:T(8,128)}, f32[128,128]{1,0:T(8,128)}, f32[256,128]{1,0:T(8,128)}, /...) custom-call(bf16[32,56,128]{2,1,0:T(8,128)(2,1)S(1)} %all_to_all.21.recv_re, ...), custom_call_target="tpu_custom_call" | custom-call | tf_op jit(solution)/shard_map/finish/pallas_call | solution.py:355
  (10 shorter events, 0.1 us)
Async XLA Ops:
  1.9 3.9 %collective-permute-start = (bf16[64,128]{1,0:T(8,128)(2,1)S(1)}, bf16[64,128]{1,0:T(8,128)(2,1)S(1)}, u32[]{:S(2)}, u32[]{:S(2)}) collective-permute-start(bf16[64,128]{1,0:T(8,128)(2,1)S(1)} %faces.1), channel_id=1, source_target_pairs={{8,16},{24,32},{40,48},{56,64},{72,80},{88,96},{104,112},{120,128}... | collective-permute-start | bytes 49160 | tf_op jit(solution)/shard_map/ppermute | solution.py:394

commit v6 on v5

--- a/solution.py
+++ b/solution.py
@@ -78,23 +78,23 @@
     out_ref[...] = picked_rows(node_ref[...], bound_ref, pick_ref, lax.axis_index("y0")).astype(BF16)
 
 
-def send_kernel(count_ref, intra_ref, bound_ref, pick_ref, *refs):
+def send_kernel(count_ref, *refs):
     arrays = (len(refs) - 4) // 2
     far, near, sem = refs[:arrays], refs[arrays + 3 : -1], refs[-1]
     out_ref, count_out_ref, onward_ref = refs[arrays : arrays + 3]
     copies = [pltpu.make_async_copy(far[k], near[k], sem.at[k]) for k in range(arrays)]
     for copy in copies:
         copy.start()
-    node_ref, second_ref, coarse_cot_ref = near[0:3]
+    node_ref, second_ref, coarse_cot_ref, intra_ref, bound_ref, pick_ref = near[0:6]
     count_out_ref[...] = jnp.full(count_out_ref.shape, count_ref[0, 0], jnp.int32)
+    for copy in copies[0:6]:
+        copy.wait()
     slab = slab_in_plane()
     last = lax.axis_size("y1") * lax.axis_size("y0") - 1
     half_rows = onward_ref.shape[0] // 2
     for k, reader in ((0, last), (1, 0)):
         column = jnp.where(slab == reader, column_of(pick_ref[1 - k]), -1)
         onward_ref[half_rows * k : half_rows * (k + 1), :] = onehot_rows(column, 128)
-    for copy in copies[0:3]:
-        copy.wait()
     odd = lax.axis_index("y0")
     node = node_ref[...]
     cells, feature = node.shape
@@ -115,7 +115,7 @@
     ]
     out_ref[pl.ds(peers * odd, peers)] = jnp.concatenate(same, axis=1).astype(BF16)
     out_ref[pl.ds(peers * (1 - odd), peers)] = jnp.concatenate(other, axis=1).astype(BF16)
-    for copy in copies[3:]:
+    for copy in copies[6:]:
         copy.wait()
 
 
@@ -398,15 +398,15 @@
 
     passed = swap(call(face_kernel, face, node, bound, pick, held=range(3), name="faces"))
     far = (
-        node, second, coarse_cot, src, dst, edge_w1, edge_b1[None], edges, edge_w2, edge_gain[None],
-        node_w1, node_b1[None], node_w2, node_gain[None], first, match, edge_cot, intra, bound, pick,
+        node, second, coarse_cot, intra, bound, pick, src, dst, edge_w1, edge_b1[None], edges, edge_w2,
+        edge_gain[None], node_w1, node_b1[None], node_w2, node_gain[None], first, match, edge_cot,
     )
     sent, count, onward_pick, *near = call(
         send_kernel,
         (shape_of((2 * peers, FIRST, feature), BF16), shape_of((8, 128), jnp.int32), shape_of((16 * peers, 128), BF16))
         + tuple(shape_of(x.shape, x.dtype) for x in far),
-        edge_count, intra, bound, pick, *far,
-        smem=(0,), held=range(1, 4), hbm=range(4, 4 + len(far)),
+        edge_count, *far,
+        smem=(0,), hbm=range(1, 1 + len(far)),
         scratch=[pltpu.SemaphoreType.DMA((len(far),))],
         name="send",
         cost=pl.CostEstimate(flops=60_000_000, bytes_accessed=400_000, transcendentals=0),
@@ -425,7 +425,7 @@
             shape_of((cells, feature), BF16),
             shape_of((in_plane * peers, HEAD + GRAD_ROWS // (in_plane * peers), feature), BF16),
         ),
-        count, received, *near[:-3],
+        count, received, *near[0:3], *near[6:],
         hbm_out=(0, 1),
         scratch=[
             pltpu.VMEM((slots, feature), BF16),
@@ -467,7 +467,7 @@
             shape_of((feature, feature), F32),
             row, row, row, row,
         ),
-        received, by_plane, d_node, fresh, *near[-3:], near[14], near[1], grads.reshape(GRAD_ROWS, feature),
+        received, by_plane, d_node, fresh, *near[3:6], near[17], near[1], grads.reshape(GRAD_ROWS, feature),
         name="finish",
     )
     return (

time: 77.8 us -> 77.8 us (level)
  no operation moved by 1% of the time
where the time goes in v6:
time: 77.8 us; the launch traced here: 77.5 us
  blocking collectives  63 us (81%)
  Pallas kernels  12.1 us (16%)
  between operations  1.4 us (2%)
    all_to_all x4, blocking collectives, exchange(): return lax.all_to_all(blocks, axes, split_axis=0, concat_axis=0, tiled=True)  63 us
    pallas_call x4, Pallas kernels, call(): pl.pallas_call(kernel, out_shape=out_shape, in_specs=[pl.BlockSpec(memory...  12.1 us
  transfers between devices with their start and end apart: 1, of which 0 were waited for; matrix products, arithmetic and copies ran while one was open for 0% of the time, Pallas kernels for 0%

profile of v6, /device:TPU:1, one launch (start us, length us, event | category | flops | bytes accessed | tf_op | source)
XLA Modules:
  0.0 77.5 jit_solution(16326107500276376539)
XLA Ops:
  0.6 1.2 %faces.1 = bf16[64,128]{1,0:T(8,128)(2,1)S(1)} custom-call(bf16[512,128]{1,0:T(8,128)(2,1)} %bitcast.33, s32[2,16]{1,0:T(2,128)} %bitcast.43, s32[2,8,8]{2,1,0:T(8,128)} %bitcast.36), custom_call_target="tpu_custom_call" | custom-call | tf_op jit(solution)/shard_map/faces/pallas_call | solution.py:355
  1.9 0.7 collective-permute-start
  3.2 1.8 %send.1 = (bf16[16,32,128]{2,1,0:T(8,128)(2,1)S(1)}, s32[8,128]{1,0:T(8,128)S(1)}, bf16[128,128]{1,0:T(8,128)(2,1)S(1)}, bf16[512,128]{1,0:T(8,128)(2,1)S(1)}, s...) custom-call(s32[1,1]{1,0:T(1,128)S(6)} %copy.33.count_ref, ...), custom_call_target="tpu_custom_call" | custom-call | flops 60000000 | bytes 400000 | tf_op jit(solution)/shard_map/send/pallas_call | solution.py:355
  5.0 0.0 collective-permute-done
  5.1 15.5 %all_to_all.20.recv_ref = bf16[16,32,128]{2,1,0:T(8,128)(2,1)S(1)} all-to-all(bf16[16,32,128]{2,1,0:T(8,128)(2,1)S(1)} %pad_maximum_fusion), channel_id=1, replica_groups=mesh['z'=8,'y1'=2,'y0'=2,'sub'=8] {'y0','sub'}, dimensions={0} | all-to-all | bytes 262144 | tf_op jit(solution)/shard_map/all_to_all | solution.py:397
  20.6 7.5 %layer.1 = (bf16[2048,128]{1,0:T(8,128)(2,1)}, bf16[2048,128]{1,0:T(8,128)(2,1)}, f32[512,128]{1,0:T(8,128)S(1)}, bf16[512,128]{1,0:T(8,128)(2,1)S(1)}, bf16[32,56,128]{2,1,0:T(8,128)(2,1)S(1)}) custom-call(s32[8,128]{1,0:T(8,128)S(1)} %get-tuple-element.50.count_ref, bf16[16,32,128]{2,1,0:T(8,128)(2,1)S(1)} %all_to_all.20.recv_ref, ...), custom_call_target="tpu_custom_call" | custom-call | tf_op jit(solution)/shard_map/layer/pallas_call | solution.py:355
  28.1 17.9 %all_to_all.21.recv_ref = bf16[32,56,128]{2,1,0:T(8,128)(2,1)S(1)} all-to-all(bf16[32,56,128]{2,1,0:T(8,128)(2,1)S(1)} %get-tuple-element.70), channel_id=1, replica_groups=mesh['z'=8,'y1'=2,'y0'=2,'sub'=8] {'y1','y0','sub'}, dimensions={0} | all-to-all | bytes 917504 | tf_op jit(solution)/shard_map/all_to_all | solution.py:397
  45.9 0.2 fusion
  46.1 0.1 slice_reduce_fusion
  46.2 15.4 %all_to_all.22.planes_ref = bf16[8,48,128]{2,1,0:T(8,128)(2,1)S(1)} all-to-all(bf16[8,48,128]{2,1,0:T(8,128)(2,1)S(1)} %broadcast_in_dim.35), channel_id=1, replica_groups=mesh['z'=8,'y1'=2,'y0'=2,'sub'=8] {'z'}, dimensions={0} | all-to-all | bytes 196608 | tf_op jit(solution)/shard_map/all_to_all | solution.py:397
  61.7 14.2 %all_to_all.23 = bf16[32,32,128]{2,1,0:T(8,128)(2,1)S(1)} all-to-all(bf16[32,32,128]{2,1,0:T(8,128)(2,1)S(1)} %broadcast_in_dim.36), channel_id=1, replica_groups=mesh['z'=8,'y1'=2,'y0'=2,'sub'=8] {'y1','y0','sub'}, dimensions={0} | all-to-all | bytes 524288 | tf_op jit(solution)/shard_map/all_to_all | solution.py:397
  75.9 1.6 %finish.1 = (f32[512,128]{1,0:T(8,128)}, bf16[256,128]{1,0:T(8,128)(2,1)}, f32[384,128]{1,0:T(8,128)}, f32[128,128]{1,0:T(8,128)}, f32[256,128]{1,0:T(8,128)}, /...) custom-call(bf16[32,56,128]{2,1,0:T(8,128)(2,1)S(1)} %all_to_all.21.recv_re, ...), custom_call_target="tpu_custom_call" | custom-call | tf_op jit(solution)/shard_map/finish/pallas_call | solution.py:355
  (10 shorter events, 0.1 us)
Async XLA Ops:
  1.9 3.1 %collective-permute-start = (bf16[64,128]{1,0:T(8,128)(2,1)S(1)}, bf16[64,128]{1,0:T(8,128)(2,1)S(1)}, u32[]{:S(2)}, u32[]{:S(2)}) collective-permute-start(bf16[64,128]{1,0:T(8,128)(2,1)S(1)} %faces.1), channel_id=1, source_target_pairs={{8,16},{24,32},{40,48},{56,64},{72,80},{88,96},{104,112},{120,128}... | collective-permute-start | bytes 49160 | tf_op jit(solution)/shard_map/ppermute | solution.py:394

commit v7 on v6

--- a/solution.py
+++ b/solution.py
@@ -215,8 +215,7 @@
     new_edges_ref[...] = new_edges.astype(BF16)
     edges_copy = pltpu.make_async_copy(new_edges_ref, new_edges_out, out_sem.at[0])
     edges_copy.start()
-    both = mm_nt(jnp.concatenate(two_parts(message), axis=0), oht_ref[wide:, :])
-    aggregate = (both[0:feature] + both[feature:]).T.astype(BF16)
+    aggregate = mm_nt(message.astype(BF16), oht_ref[wide:, :]).T.astype(BF16)
 
     nw1_node = nw1_ref[0:feature, :]
     nw1_agg = nw1_ref[feature:, :]

time: 77.8 us -> 77.7 us (level)
  no operation moved by 1% of the time
where the time goes in v7:
time: 77.7 us; the launch traced here: 77.4 us
  blocking collectives  63 us (81%)
  Pallas kernels  12 us (15%)
  between operations  1.4 us (2%)
    all_to_all x4, blocking collectives, exchange(): return lax.all_to_all(blocks, axes, split_axis=0, concat_axis=0, tiled=True)  63 us
    pallas_call x4, Pallas kernels, call(): pl.pallas_call(kernel, out_shape=out_shape, in_specs=[pl.BlockSpec(memory...  12 us
  transfers between devices with their start and end apart: 1, of which 0 were waited for; matrix products, arithmetic and copies ran while one was open for 0% of the time, Pallas kernels for 0%

profile of v7, /device:TPU:1, one launch (start us, length us, event | category | flops | bytes accessed | tf_op | source)
XLA Modules:
  0.0 77.4 jit_solution(16891864056260000033)
XLA Ops:
  0.6 1.2 %faces.1 = bf16[64,128]{1,0:T(8,128)(2,1)S(1)} custom-call(bf16[512,128]{1,0:T(8,128)(2,1)} %bitcast.33, s32[2,16]{1,0:T(2,128)} %bitcast.43, s32[2,8,8]{2,1,0:T(8,128)} %bitcast.36), custom_call_target="tpu_custom_call" | custom-call | tf_op jit(solution)/shard_map/faces/pallas_call | solution.py:354
  1.9 0.7 collective-permute-start
  3.2 1.8 %send.1 = (bf16[16,32,128]{2,1,0:T(8,128)(2,1)S(1)}, s32[8,128]{1,0:T(8,128)S(1)}, bf16[128,128]{1,0:T(8,128)(2,1)S(1)}, bf16[512,128]{1,0:T(8,128)(2,1)S(1)}, s...) custom-call(s32[1,1]{1,0:T(1,128)S(6)} %copy.33.count_ref, ...), custom_call_target="tpu_custom_call" | custom-call | flops 60000000 | bytes 400000 | tf_op jit(solution)/shard_map/send/pallas_call | solution.py:354
  5.0 0.0 collective-permute-done
  5.1 15.5 %all_to_all.20.recv_ref = bf16[16,32,128]{2,1,0:T(8,128)(2,1)S(1)} all-to-all(bf16[16,32,128]{2,1,0:T(8,128)(2,1)S(1)} %pad_maximum_fusion), channel_id=1, replica_groups=mesh['z'=8,'y1'=2,'y0'=2,'sub'=8] {'y0','sub'}, dimensions={0} | all-to-all | bytes 262144 | tf_op jit(solution)/shard_map/all_to_all | solution.py:396
  20.6 7.4 %layer.1 = (bf16[2048,128]{1,0:T(8,128)(2,1)}, bf16[2048,128]{1,0:T(8,128)(2,1)}, f32[512,128]{1,0:T(8,128)S(1)}, bf16[512,128]{1,0:T(8,128)(2,1)S(1)}, bf16[32,56,128]{2,1,0:T(8,128)(2,1)S(1)}) custom-call(s32[8,128]{1,0:T(8,128)S(1)} %get-tuple-element.50.count_ref, bf16[16,32,128]{2,1,0:T(8,128)(2,1)S(1)} %all_to_all.20.recv_ref, ...), custom_call_target="tpu_custom_call" | custom-call | tf_op jit(solution)/shard_map/layer/pallas_call | solution.py:354
  28.0 17.9 %all_to_all.21.recv_ref = bf16[32,56,128]{2,1,0:T(8,128)(2,1)S(1)} all-to-all(bf16[32,56,128]{2,1,0:T(8,128)(2,1)S(1)} %get-tuple-element.70), channel_id=1, replica_groups=mesh['z'=8,'y1'=2,'y0'=2,'sub'=8] {'y1','y0','sub'}, dimensions={0} | all-to-all | bytes 917504 | tf_op jit(solution)/shard_map/all_to_all | solution.py:396
  45.8 0.2 fusion
  46.0 0.1 slice_reduce_fusion
  46.1 15.4 %all_to_all.22.planes_ref = bf16[8,48,128]{2,1,0:T(8,128)(2,1)S(1)} all-to-all(bf16[8,48,128]{2,1,0:T(8,128)(2,1)S(1)} %broadcast_in_dim.35), channel_id=1, replica_groups=mesh['z'=8,'y1'=2,'y0'=2,'sub'=8] {'z'}, dimensions={0} | all-to-all | bytes 196608 | tf_op jit(solution)/shard_map/all_to_all | solution.py:396
  61.6 14.2 %all_to_all.23 = bf16[32,32,128]{2,1,0:T(8,128)(2,1)S(1)} all-to-all(bf16[32,32,128]{2,1,0:T(8,128)(2,1)S(1)} %broadcast_in_dim.36), channel_id=1, replica_groups=mesh['z'=8,'y1'=2,'y0'=2,'sub'=8] {'y1','y0','sub'}, dimensions={0} | all-to-all | bytes 524288 | tf_op jit(solution)/shard_map/all_to_all | solution.py:396
  75.8 1.6 %finish.1 = (f32[512,128]{1,0:T(8,128)}, bf16[256,128]{1,0:T(8,128)(2,1)}, f32[384,128]{1,0:T(8,128)}, f32[128,128]{1,0:T(8,128)}, f32[256,128]{1,0:T(8,128)}, /...) custom-call(bf16[32,56,128]{2,1,0:T(8,128)(2,1)S(1)} %all_to_all.21.recv_re, ...), custom_call_target="tpu_custom_call" | custom-call | tf_op jit(solution)/shard_map/finish/pallas_call | solution.py:354
  (10 shorter events, 0.1 us)
Async XLA Ops:
  1.9 3.1 %collective-permute-start = (bf16[64,128]{1,0:T(8,128)(2,1)S(1)}, bf16[64,128]{1,0:T(8,128)(2,1)S(1)}, u32[]{:S(2)}, u32[]{:S(2)}) collective-permute-start(bf16[64,128]{1,0:T(8,128)(2,1)S(1)} %faces.1), channel_id=1, source_target_pairs={{8,16},{24,32},{40,48},{56,64},{72,80},{88,96},{104,112},{120,128}... | collective-permute-start | bytes 49160 | tf_op jit(solution)/shard_map/ppermute | solution.py:393
